TPU v7x, 512 devices: a whole 4x8x8 slice. The times are simulated.
512 devices in a mesh: ctx: 64 (over x, y_hi, z), tp: 8 (over y_lo, core).
Axes of the slice: x: 4, y: 8 (y_hi: 2, y_lo: 4; y = y_hi * 4 + y_lo), z: 8, core: 2. Of those that a mesh axis runs over, the one named last changes fastest.
Arguments:
- q_proj: bfloat16 [8192, 4096], P('ctx', 'tp'), may hold values from -6 to 6
- k_proj: bfloat16 [8192, 4096], P('ctx', 'tp'), may hold values from -6 to 6
- v_proj: bfloat16 [8192, 4096], P('ctx', 'tp'), may hold values from -6 to 6
- short_taps: float32 [3, 3, 4096], P(None, None, 'tp'), may hold values from -3.5 to 3.5
- long_filter: float32 [8192, 4096], P('ctx', 'tp'), may hold values from -1.01 to 1.01
- grad_out: bfloat16 [8192, 4096], P('ctx', 'tp'), may hold values from -1.1953125 to 1.1953125
Outputs:
- mixed: bfloat16 [8192, 4096], P('ctx', 'tp')
- grad_q: bfloat16 [8192, 4096], P('ctx', 'tp')
- grad_k: bfloat16 [8192, 4096], P('ctx', 'tp')
- grad_v: bfloat16 [8192, 4096], P('ctx', 'tp')
- grad_taps: float32 [3, 3, 4096], P(None, None, 'tp')
- grad_filter: float32 [8192, 4096], P('ctx', 'tp')
All inputs are finite; a program needn't handle non-finite values.
Results may differ from a plain program's by a relative error of at most 0.0015.
Values may be sent and summed in bfloat16 or wider, within the bound.
A program may use at most 64 MiB of HBM per device.

v0:
```python
import math

import jax
import jax.numpy as jnp
from jax import lax
from jax.sharding import PartitionSpec as P


def passed_along(value, axis, steps):
    count = lax.axis_size(axis)
    initial, last = (max(0, -steps), min(count, count - steps))
    return lax.ppermute(value, axis, [(source, source + steps) for source in range(initial, last)])


def angles(first, second, period):
    product = first[:, None] * second[None, :] % period
    return product.astype(jnp.float32) * (2.0 * math.pi / period)


def mix(table, field, form):
    return jnp.einsum(form, table, field, precision=lax.Precision.HIGHEST)


def rotate(real, imag, freqs, lags, period, sign):
    theta = angles(freqs, lags, period)[:, :, None, None]
    cosine = jnp.cos(theta)
    sine = sign * jnp.sin(theta)
    return (real * cosine - imag * sine, imag * cosine + real * sine)


def rows_transform(real, imag, sign):
    count = real.shape[1]
    theta = angles(jnp.arange(count, dtype=jnp.int32), jnp.arange(count, dtype=jnp.int32), count)
    cosine = jnp.cos(theta)
    sine = sign * jnp.sin(theta)
    form = "kt,atfc->akfc"
    out_real = mix(cosine, real, form) - mix(sine, imag, form)
    out_imag = mix(cosine, imag, form) + mix(sine, real, form)
    return (out_real, out_imag)


def coarse_tables(parts, factor):
    coarse = jnp.arange(parts, dtype=jnp.int32)
    theta = angles(coarse, coarse, 2 * parts)
    weight = jnp.where(coarse == 0, 1.0, factor).astype(jnp.float32)[:, None]
    signs = jnp.where(coarse % 2 == 0, 1.0, -1.0).astype(jnp.float32)
    cos_table = jnp.cos(theta) * weight
    sin_table = jnp.concatenate([signs[None], -factor * jnp.sin(theta)[1:]], axis=0)
    return (cos_table, sin_table)


def half_forward(fields):
    parts = lax.axis_size("ctx")
    rows = fields.shape[0]
    count = fields.shape[1]
    period = 2 * parts * rows
    lanes = lax.all_to_all(fields[None], "ctx", split_axis=1, concat_axis=0, tiled=True)
    block = rows // parts
    place = lax.axis_index("ctx")
    lags = place * block + jnp.arange(block, dtype=jnp.int32)
    cos_table, sin_table = coarse_tables(parts, 1.0)
    real = mix(cos_table, lanes, "kp,pbfc->kbfc")
    imag = mix(sin_table, lanes, "kp,pbfc->kbfc")
    real, imag = rotate(real, imag, jnp.arange(parts, dtype=jnp.int32), lags, period, -1.0)
    packed = jnp.concatenate([real, imag], axis=2)
    packed = lax.all_to_all(packed, "ctx", split_axis=0, concat_axis=1, tiled=True)
    own_re = packed[0, :, :count]
    own_im = packed[0, :, count:]
    first = place == 0
    ones = jnp.ones((1,), jnp.int32)
    positions = jnp.arange(rows, dtype=jnp.int32)
    full_turn = angles(ones, positions, rows)[0][:, None, None]
    half_turn = angles(ones, positions, 2 * rows)[0][:, None, None]
    partner_re = jnp.where(
        first,
        own_im * jnp.cos(half_turn),
        own_re * jnp.cos(full_turn) - own_im * jnp.sin(full_turn),
    )
    partner_im = jnp.where(
        first,
        -own_im * jnp.sin(half_turn),
        -(own_re * jnp.sin(full_turn) + own_im * jnp.cos(full_turn)),
    )
    lead_im = jnp.where(first, jnp.zeros_like(own_im), own_im)
    real = jnp.stack([own_re, partner_re], axis=0)
    imag = jnp.stack([lead_im, partner_im], axis=0)
    return rows_transform(real, imag, -1.0)


def half_inverse(real, imag):
    parts = lax.axis_size("ctx")
    rows = real.shape[1]
    count = real.shape[2]
    period = 2 * parts * rows
    scale = 1.0 / period
    real, imag = rows_transform(real, imag, 1.0)
    place = lax.axis_index("ctx")
    first = place == 0
    freqs = jnp.stack([place, jnp.where(first, parts, 2 * parts - place)])
    real, imag = rotate(real, imag, freqs, jnp.arange(rows, dtype=jnp.int32), period, 1.0)
    send_im = jnp.where(first, real[1], imag[0])
    packed = jnp.concatenate([real[0], send_im], axis=1)[None]
    packed = lax.all_to_all(packed, "ctx", split_axis=1, concat_axis=0, tiled=True)
    cos_table, sin_table = coarse_tables(parts, 2.0)
    lanes = (
        mix(cos_table, packed[:, :, :count], "kp,kbfc->pbfc")
        + mix(sin_table, packed[:, :, count:], "kp,kbfc->pbfc")
    ) * scale
    back = lax.all_to_all(lanes, "ctx", split_axis=0, concat_axis=1, tiled=True)
    return back[0]


def spectrum(fields):
    return half_forward(fields)


def signal(real, imag):
    return half_inverse(real, imag)


def local(q_proj, k_proj, v_proj, short_taps, long_filter, grad_out):
    rows = q_proj.shape[0]
    taps = short_taps.shape[1]
    reach = taps - 1
    before = passed_along(
        (q_proj[rows - reach :], k_proj[rows - reach :], v_proj[rows - reach :]), "ctx", 1
    )
    inputs = (q_proj, k_proj, v_proj)
    extended = []
    featured = []
    for s in range(3):
        joined = jnp.concatenate([before[s], inputs[s]], axis=0).astype(jnp.float32)
        extended.append(joined)
        total = jnp.zeros((rows, joined.shape[1]), jnp.float32)
        for j in range(taps):
            total = total + short_taps[s, j][None, :] * joined[reach - j : reach - j + rows]
        featured.append(total)
    z = featured[0] * featured[2]
    grad = grad_out.astype(jnp.float32)
    gy = grad * featured[1]
    fields = jnp.stack([z, long_filter, gy], axis=1)
    real, imag = spectrum(fields)
    z_re, z_im = (real[:, :, 0], imag[:, :, 0])
    h_re, h_im = (real[:, :, 1], imag[:, :, 1])
    g_re, g_im = (real[:, :, 2], imag[:, :, 2])
    out_real = jnp.stack(
        [z_re * h_re - z_im * h_im, g_re * h_re + g_im * h_im, g_re * z_re + g_im * z_im], axis=2
    )
    out_imag = jnp.stack(
        [z_re * h_im + z_im * h_re, g_im * h_re - g_re * h_im, g_im * z_re - g_re * z_im], axis=2
    )
    results = signal(out_real, out_imag)
    y = results[:, 0]
    dz = results[:, 1]
    grad_filter = results[:, 2]
    mixed = (featured[1] * y).astype(jnp.bfloat16)
    deltas = (dz * featured[2], grad * y, dz * featured[0])
    after = passed_along((deltas[0][:reach], deltas[1][:reach], deltas[2][:reach]), "ctx", -1)
    grads = []
    tap_rows = []
    for s in range(3):
        joined = jnp.concatenate([deltas[s], after[s]], axis=0)
        total = jnp.zeros((rows, joined.shape[1]), jnp.float32)
        pieces = []
        for j in range(taps):
            total = total + short_taps[s, j][None, :] * joined[j : j + rows]
            pieces.append(jnp.sum(deltas[s] * extended[s][reach - j : reach - j + rows], axis=0))
        grads.append(total.astype(jnp.bfloat16))
        tap_rows.append(jnp.stack(pieces, axis=0))
    local_taps = jnp.stack(tap_rows, axis=0)
    grad_taps = lax.psum(local_taps, "ctx")
    return (mixed, grads[0], grads[1], grads[2], grad_taps, grad_filter)


def solution(mesh):
    return jax.shard_map(
        local,
        mesh=mesh,
        in_specs=(
            P("ctx", "tp"),
            P("ctx", "tp"),
            P("ctx", "tp"),
            P(None, None, "tp"),
            P("ctx", "tp"),
            P("ctx", "tp"),
        ),
        out_specs=(
            P("ctx", "tp"),
            P("ctx", "tp"),
            P("ctx", "tp"),
            P("ctx", "tp"),
            P(None, None, "tp"),
            P("ctx", "tp"),
        ),
        check_vma=False,
    )
```

profile of v0, /device:TPU:64, one launch (start us, length us, event | category | flops | bytes accessed | tf_op | source)
XLA Modules:
  0.0 678.5 jit_solution(12162808788412787277)
XLA Ops:
  1.4 4.3 collective-permute-start.1
  6.4 4.3 collective-permute-start.2
  11.4 5.5 collective-permute-start
  19.1 1.7 fusion.28
  21.8 1.7 copy.43
  23.5 16.3 %all-to-all-start = ((f32[1,128,3,512]{3,0,2,1:T(1,128)}), f32[1,128,3,512]{3,0,2,1:T(1,128)S(1)}, u32[]{:S(2)}, u32[]{:S(2)}) async-start(f32[1,128,3,512]{3,0,2,1:T(1,128)} %copy.43), calls=%async_computation | async-start | bytes 1572864 | tf_op jit(solution)/shard_map/all_to_all | solution.py:57
  40.2 21.7 %all-to-all-done = f32[1,128,3,512]{3,0,2,1:T(1,128)S(1)} async-done(((f32[1,128,3,512]{3,0,2,1:T(1,128)}), f32[1,128,3,512]{3,0,2,1:T(1,128)S(1)}, u32[]{:S(2)}, u32[]{:S(2)}) %all-to-all-start) | async-done | bytes 786464 | tf_op jit(solution)/shard_map/all_to_all | solution.py:57
  63.4 1.4 multiply_subtract_fusion
  64.9 2.4 copy.47
  67.3 9.6 %all-to-all-start.1 = ((f32[64,2,6,512]{3,1,2,0:T(2,128)}), f32[64,2,6,512]{3,1,2,0:T(2,128)S(1)}, u32[]{:S(2)}, u32[]{:S(2)}) async-start(f32[64,2,6,512]{3,1,2,0:T(2,128)} %copy.47), calls=%async_computation.1 | async-start | bytes 3145728 | tf_op jit(solution)/shard_map/all_to_all | solution.py:66
  77.2 42.0 %all-to-all-done.1 = f32[64,2,6,512]{3,1,2,0:T(2,128)S(1)} async-done(((f32[64,2,6,512]{3,1,2,0:T(2,128)}), f32[64,2,6,512]{3,1,2,0:T(2,128)S(1)}, u32[]{:S(2)}, u32[]{:S(2)}) %all-to-all-start.1) | async-done | bytes 1572896 | tf_op jit(solution)/shard_map/all_to_all | solution.py:66
  119.2 1.7 copy.48
  120.9 2.5 all_to_all.17
  124.5 1.4 copy.74
  126.5 1.7 fusion.2
  128.2 1.6 fusion.1
  129.9 1.7 subtract_bitcast_fusion.1
  131.6 1.7 add_bitcast_fusion.1
  133.6 1.7 fusion.4
  135.3 1.7 fusion.3
  137.0 1.9 convolution_add_fusion
  138.9 2.0 subtract_bitcast_fusion
  141.2 2.9 copy.51
  144.1 8.6 %all-to-all-start.2 = ((f32[1,128,6,512]{3,0,2,1:T(1,128)}), f32[1,128,6,512]{3,0,2,1:T(1,128)S(1)}, u32[]{:S(2)}, u32[]{:S(2)}) async-start(f32[1,128,6,512]{3,0,2,1:T(1,128)} %copy.51), calls=%async_computation.2 | async-start | bytes 3145728 | tf_op jit(solution)/shard_map/all_to_all | solution.py:103
  152.7 41.7 %all-to-all-done.2 = f32[1,128,6,512]{3,0,2,1:T(1,128)S(1)} async-done(((f32[1,128,6,512]{3,0,2,1:T(1,128)}), f32[1,128,6,512]{3,0,2,1:T(1,128)S(1)}, u32[]{:S(2)}, u32[]{:S(2)}) %all-to-all-start.2) | async-done | bytes 1572896 | tf_op jit(solution)/shard_map/all_to_all | solution.py:103
  195.4 1.3 fusion.7
  198.6 33.0 %all_to_all.45 = f32[64,2,3,512]{3,1,2,0:T(2,128)S(1)} all-to-all(f32[64,2,3,512]{3,1,2,0:T(2,128)S(1)} %copy.57), channel_id=1, replica_groups=mesh['ctx'=64,'tp'=8] {'ctx'}, dimensions={0} | all-to-all | bytes 1572864 | tf_op jit(solution)/shard_map/all_to_all | solution.py:109
  234.1 3.1 collective-permute-start.5
  237.2 422.8 %psum.7 = f32[3,3,512]{2,1,0:T(4,128)} all-reduce(f32[3,3,512]{2,1,0:T(4,128)S(1)} %pad_maximum_fusion.18), channel_id=1, replica_groups=mesh['ctx'=64,'tp'=8] {'ctx'}, use_global_device_ids=true, to_apply=%region_9.10 | all-reduce | flops 4608 | bytes 36864 | tf_op jit(solution)/shard_map/psum | solution.py:171
  660.0 12.3 %collective-permute-start.4 = (f32[2,512]{1,0:T(2,128)S(1)}, f32[2,512]{1,0:T(2,128)S(1)}, u32[]{:S(2)}, u32[]{:S(2)}) collective-permute-start(f32[2,512]{1,0:T(2,128)S(1)} %slice.237), channel_id=1, source_target_pairs={{8,0},{16,8},{24,16},{32,24},{40,32},{48,40},{56,48},{64,56},{72,6... | collective-permute-start | bytes 12296 | tf_op jit(solution)/shard_map/ppermute | solution.py:12
  672.3 1.9 collective-permute-start.3
  675.7 2.1 collective-permute-done.3
  (64 shorter events, 17.5 us)
Async XLA Ops:
  0.6 20.2 %copy-start.4 = (bf16[128,512]{1,0:T(8,128)(2,1)S(1)}, bf16[128,512]{1,0:T(8,128)(2,1)}, u32[]{:S(2)}) copy-start(bf16[128,512]{1,0:T(8,128)(2,1)} %param.6) | copy-start | bytes 393220
  0.6 20.2 %copy-start.5 = (bf16[128,512]{1,0:T(8,128)(2,1)S(1)}, bf16[128,512]{1,0:T(8,128)(2,1)}, u32[]{:S(2)}) copy-start(bf16[128,512]{1,0:T(8,128)(2,1)} %param.8) | copy-start | bytes 393220
  1.4 19.4 %collective-permute-start.1 = (bf16[2,512]{1,0:T(2,128)(2,1)S(1)}, bf16[2,512]{1,0:T(2,128)(2,1)S(1)}, u32[]{:S(2)}, u32[]{:S(2)}) collective-permute-start(bf16[2,512]{1,0:T(2,128)(2,1)S(1)} %slice.170), channel_id=1, source_target_pairs={{0,8},{8,16},{16,24},{24,32},{32,40},{40,48},{48,56},{56,64},{64,7... | collective-permute-start | bytes 6152 | tf_op jit(solution)/shard_map/ppermute | solution.py:12
  6.4 14.5 %collective-permute-start.2 = (bf16[2,512]{1,0:T(2,128)(2,1)S(1)}, bf16[2,512]{1,0:T(2,128)(2,1)S(1)}, u32[]{:S(2)}, u32[]{:S(2)}) collective-permute-start(bf16[2,512]{1,0:T(2,128)(2,1)S(1)} %slice.177), channel_id=1, source_target_pairs={{0,8},{8,16},{16,24},{24,32},{32,40},{40,48},{48,56},{56,64},{64,7... | collective-permute-start | bytes 6152 | tf_op jit(solution)/shard_map/ppermute | solution.py:12
  11.4 6.8 collective-permute-start
  20.8 1.0 copy-start.3
  23.5 38.3 %all-to-all-start = ((f32[1,128,3,512]{3,0,2,1:T(1,128)}), f32[1,128,3,512]{3,0,2,1:T(1,128)S(1)}, u32[]{:S(2)}, u32[]{:S(2)}) async-start(f32[1,128,3,512]{3,0,2,1:T(1,128)} %copy.43), calls=%async_computation | async-start | bytes 1572864 | tf_op jit(solution)/shard_map/all_to_all | solution.py:57
  67.3 51.9 %all-to-all-start.1 = ((f32[64,2,6,512]{3,1,2,0:T(2,128)}), f32[64,2,6,512]{3,1,2,0:T(2,128)S(1)}, u32[]{:S(2)}, u32[]{:S(2)}) async-start(f32[64,2,6,512]{3,1,2,0:T(2,128)} %copy.47), calls=%async_computation.1 | async-start | bytes 3145728 | tf_op jit(solution)/shard_map/all_to_all | solution.py:66
  144.1 50.3 %all-to-all-start.2 = ((f32[1,128,6,512]{3,0,2,1:T(1,128)}), f32[1,128,6,512]{3,0,2,1:T(1,128)S(1)}, u32[]{:S(2)}, u32[]{:S(2)}) async-start(f32[1,128,6,512]{3,0,2,1:T(1,128)} %copy.51), calls=%async_computation.2 | async-start | bytes 3145728 | tf_op jit(solution)/shard_map/all_to_all | solution.py:103
  231.5 1.6 copy-start
  231.5 1.6 copy-start.1
  231.5 1.6 copy-start.2
  234.1 440.2 %collective-permute-start.5 = (f32[2,512]{1,0:T(2,128)S(1)}, f32[2,512]{1,0:T(2,128)S(1)}, u32[]{:S(2)}, u32[]{:S(2)}) collective-permute-start(f32[2,512]{1,0:T(2,128)S(1)} %slice.240), channel_id=1, source_target_pairs={{8,0},{16,8},{24,16},{32,24},{40,32},{48,40},{56,48},{64,56},{72,6... | collective-permute-start | bytes 12296 | tf_op jit(solution)/shard_map/ppermute | solution.py:12
  660.0 15.0 %collective-permute-start.4 = (f32[2,512]{1,0:T(2,128)S(1)}, f32[2,512]{1,0:T(2,128)S(1)}, u32[]{:S(2)}, u32[]{:S(2)}) collective-permute-start(f32[2,512]{1,0:T(2,128)S(1)} %slice.237), channel_id=1, source_target_pairs={{8,0},{16,8},{24,16},{32,24},{40,32},{48,40},{56,48},{64,56},{72,6... | collective-permute-start | bytes 12296 | tf_op jit(solution)/shard_map/ppermute | solution.py:12
  672.3 5.5 collective-permute-start.3
where the time goes:
time: 680 us; the launch traced here: 679 us
  blocking collectives  456 us (67%)
  waiting for transfers between devices  108 us (16%)
  starting transfers between devices  65.8 us (10%)
  local copies, waits for them, and re-layouts  20.4 us (3%)
  matrix products  19.2 us (3%)
  other arithmetic  8.53 us (1%)
    psum x1, blocking collectives, local(): grad_taps = lax.psum(local_taps, 'ctx')  423 us
    all_to_all x1, waiting for transfers between devices, half_forward(): lax.all_to_all(packed, 'ctx', split_axis=0, concat_axis=1, tiled=True)  42 us
    all_to_all x1, waiting for transfers between devices, half_inverse(): lax.all_to_all(packed, 'ctx', split_axis=1, concat_axis=0, tiled=True)  41.7 us
    all_to_all x1, blocking collectives, half_inverse(): back = lax.all_to_all(lanes, 'ctx', split_axis=0, concat_axis=1, tiled=True)  33 us
    ppermute x6, starting transfers between devices, passed_along(): lax.ppermute(value, axis, [(source, source + steps) for source in range(i...  31.3 us
    all_to_all x1, waiting for transfers between devices, half_forward(): lax.all_to_all(fields[None], 'ctx', split_axis=1, concat_axis=0, tiled=True)  21.7 us
    dot_general x12, matrix products, mix(): return jnp.einsum(form, table, field, precision=lax.Precision.HIGHEST)  19.2 us
    all_to_all x1, starting transfers between devices, half_forward(): lax.all_to_all(fields[None], 'ctx', split_axis=1, concat_axis=0, tiled=True)  16.3 us
  transfers between devices with their start and end apart: 9, of which 5 were waited for; matrix products, arithmetic and copies ran while one was open for 1% of the time, Pallas kernels for 0%

commit v1 on v0

v1 whole, which is shorter than its diff:
```python
import math

import jax
import jax.numpy as jnp
import numpy as np
from jax import lax
from jax.experimental import pallas as pl
from jax.experimental.pallas import tpu as pltpu
from jax.sharding import PartitionSpec as P

F32 = jnp.float32
BF16 = jnp.bfloat16


def split_table(table):
    hi = table.astype(BF16)
    return hi, (table - hi.astype(np.float64)).astype(BF16)


def make_tables(parts, rows):
    total = parts * rows
    k1 = np.arange(parts)
    p = np.arange(parts)
    t = np.arange(rows)
    coarse = 2.0 * math.pi * np.outer(k1 + 0.25, p) / parts
    first = np.concatenate([np.cos(coarse), -np.sin(coarse)], axis=0)
    hi, lo = split_table(first)
    first = np.concatenate([hi, hi, lo], axis=1)
    turn = 2.0 * math.pi * np.outer(k1 + 0.25, t) / total
    fine = 2.0 * math.pi * (np.outer(t, t) % rows) / rows
    second = np.block([[np.cos(fine), -np.sin(fine)], [np.sin(fine), np.cos(fine)]])
    hi, lo = split_table(second)
    second = np.concatenate([hi, hi, lo], axis=0)
    last = np.concatenate([np.cos(coarse.T), np.sin(coarse.T)], axis=1) / total
    hi, lo = split_table(last)
    last = np.concatenate([hi, hi, lo], axis=1)
    return first, second, last, np.cos(turn).astype(np.float32), -np.sin(turn).astype(np.float32)


def halves(value):
    hi = value.astype(BF16)
    return hi, (value - hi.astype(F32)).astype(BF16)


def kernel(
    q_ref, k_ref, v_ref, g_ref, h_ref, taps_ref, first_ref, second_ref, last_ref, cos_ref, sin_ref,
    mixed_ref, gq_ref, gk_ref, gv_ref, gtaps_ref, gh_ref,
    send, recv, send2, recv2, taps_t, x, feat, fields, spec, conv, lhs,
    send_sem, recv_sem, send_sem2, recv_sem2,
):
    parts, chans, rows = 64, 8, 128
    width = parts * chans
    me = lax.axis_index("ctx")
    tp = lax.axis_index("tp")
    barrier = pltpu.get_barrier_semaphore()

    def peers(body):
        def step(i, carry):
            body(jnp.bitwise_xor(me, i))
            return carry

        lax.fori_loop(1, parts, step, 0)

    def target(peer):
        return dict(device_id=(peer, tp), device_id_type=pl.DeviceIdType.MESH)

    peers(lambda peer: pl.semaphore_signal(barrier, inc=1, **target(peer)))

    def turned(ref):
        return jnp.transpose(ref[...].astype(F32)).reshape(parts, chans, rows)

    send[:, 0:16, :] = jnp.concatenate([turned(q_ref), turned(k_ref)], axis=1).astype(BF16)
    send[:, 16:32, :] = jnp.concatenate([turned(v_ref), turned(g_ref)], axis=1).astype(BF16)
    filt = turned(h_ref)
    filt_hi = filt.astype(BF16).astype(F32)
    send[:, 32:48, :] = jnp.concatenate([filt_hi, filt - filt_hi], axis=1).astype(BF16)
    taps = jnp.concatenate([taps_ref[...], jnp.zeros((rows - 9, width), F32)], axis=0)
    taps_t[...] = jnp.transpose(taps)

    pl.semaphore_wait(barrier, parts - 1)
    own = pltpu.make_async_copy(send.at[me], recv.at[me], recv_sem)
    own.start()

    def post(peer):
        pltpu.make_async_remote_copy(
            src_ref=send.at[peer], dst_ref=recv.at[me], send_sem=send_sem, recv_sem=recv_sem, **target(peer)
        ).start()

    peers(post)
    pltpu.make_async_copy(recv, recv, recv_sem).wait()

    own_taps = taps_t[pl.ds(pl.multiple_of(me * chans, chans), chans), :]

    def tap(s, j):
        return jnp.broadcast_to(own_taps[:, 3 * s + j : 3 * s + j + 1], (chans, rows))[None]

    lane = lax.broadcasted_iota(jnp.int32, (1, chans, rows), 2)
    chunk = 8

    def rolled(value, shift):
        flat = value.reshape(-1, rows)
        return pltpu.roll(flat, shift % rows, axis=1).reshape(value.shape)

    x[:, 0] = jnp.zeros((4, chans, rows), F32)

    def unpack(i, carry):
        p0 = i * chunk
        here = pl.ds(p0, chunk)
        there = pl.ds(p0 + 1, chunk)
        qk = recv[here, 0:16, :].astype(F32)
        vg = recv[here, 16:32, :].astype(F32)
        hh = recv[here, 32:48, :].astype(F32)
        x[0, there] = qk[:, 0:8]
        x[1, there] = qk[:, 8:16]
        x[2, there] = vg[:, 0:8]
        x[3, there] = vg[:, 8:16]
        fields[1, here] = hh[:, 0:8] + hh[:, 8:16]
        return carry

    lax.fori_loop(0, parts // chunk, unpack, 0)

    def delayed(s, p0):
        value = x[s, pl.ds(p0, chunk + 1)]
        out = [value[1:]]
        for j in (1, 2):
            moved = rolled(value, j)
            out.append(jnp.where(lane < j, moved[:-1], moved[1:]))
        return out

    def featurize(i, carry):
        p0 = i * chunk
        here = pl.ds(p0, chunk)
        a = []
        for s in range(3):
            d = delayed(s, p0)
            a.append(tap(s, 0) * d[0] + tap(s, 1) * d[1] + tap(s, 2) * d[2])
            feat[s, here] = a[s]
        fields[0, here] = a[0] * a[2]
        fields[2, here] = a[1] * x[3, pl.ds(p0 + 1, chunk)]
        return carry

    lax.fori_loop(0, parts // chunk, featurize, 0)

    turn_re, turn_im = cos_ref[...], sin_ref[...]
    first, second, last = first_ref[...], second_ref[...], last_ref[...]
    flat_fields = fields.reshape(3 * width, rows)
    flat_conv = conv.reshape(3 * width, rows)

    def twiddled(re, im):
        return re * turn_re - im * turn_im, re * turn_im + im * turn_re

    def forward(f, carry):
        for c in range(0, chans, 2):
            pair = [flat_fields[pl.ds(f * width + c + e, parts, stride=chans), :] for e in (0, 1)]
            hi, lo = halves(jnp.concatenate(pair, axis=1))
            mid = jnp.dot(first, jnp.concatenate([hi, lo, hi], axis=0), preferred_element_type=F32)
            for e in (0, 1):
                re, im = twiddled(mid[:parts, e * rows : (e + 1) * rows], mid[parts:, e * rows : (e + 1) * rows])
                hi, lo = halves(jnp.concatenate([re, im], axis=1))
                lhs[(c + e) * parts : (c + e + 1) * parts, :] = jnp.concatenate([hi, lo, hi], axis=1)
        spec[f] = jnp.dot(lhs[...], second, preferred_element_type=F32)
        return carry

    lax.fori_loop(0, 3, forward, 0)

    def inverse(o, carry):
        f_a = jnp.where(o == 0, 0, 2)
        f_b = jnp.where(o == 2, 0, 1)
        sign = jnp.where(o == 0, 1.0, -1.0).astype(F32)
        for c in range(chans):
            block = pl.ds(c * parts, parts)
            a, b = spec[f_a, block, :], spec[f_b, block, :]
            a_re, a_im, b_re, b_im = a[:, :rows], a[:, rows:], b[:, :rows], sign * b[:, rows:]
            re, im = a_re * b_re - a_im * b_im, a_re * b_im + a_im * b_re
            hi, lo = halves(jnp.concatenate([re, -im], axis=1))
            lhs[c * parts : (c + 1) * parts, :] = jnp.concatenate([hi, lo, hi], axis=1)
        mid = jnp.dot(lhs[...], second, preferred_element_type=F32)
        for c in range(0, chans, 2):
            pair = []
            for e in (0, 1):
                block = mid[(c + e) * parts : (c + e + 1) * parts]
                pair.append(jnp.concatenate(twiddled(block[:, :rows], block[:, rows:]), axis=0))
            hi, lo = halves(jnp.concatenate(pair, axis=1))
            out = jnp.dot(last, jnp.concatenate([hi, lo, hi], axis=0), preferred_element_type=F32)
            for e in (0, 1):
                flat_conv[pl.ds(o * width + c + e, parts, stride=chans), :] = out[:, e * rows : (e + 1) * rows]
        return carry

    lax.fori_loop(0, 3, inverse, 0)

    def deliver(i, carry):
        sums, edge = carry
        p0 = (parts // chunk - 1 - i) * chunk
        here = pl.ds(p0, chunk)
        y, dz, dh = conv[0, here], conv[1, here], conv[2, here]
        grad = x[3, pl.ds(p0 + 1, chunk)]
        da = [dz * feat[2, here], grad * y, dz * feat[0, here]]
        mixed = feat[1, here] * y
        grads = []
        sums = list(sums)
        for s in range(3):
            value = jnp.concatenate([da[s], edge[s][None]], axis=0)
            total = tap(s, 0) * da[s]
            for j in (1, 2):
                moved = rolled(value, -j)
                total = total + tap(s, j) * jnp.where(lane >= rows - j, moved[1:], moved[:-1])
            grads.append(total)
            d = delayed(s, p0)
            for j in range(3):
                sums[3 * s + j] = sums[3 * s + j] + jnp.sum(da[s] * d[j], axis=0)
        send2[here, 0:16, :] = jnp.concatenate([mixed, grads[0]], axis=1).astype(BF16)
        send2[here, 16:32, :] = jnp.concatenate([grads[1], grads[2]], axis=1).astype(BF16)
        dh_hi = dh.astype(BF16).astype(F32)
        send2[here, 32:48, :] = jnp.concatenate([dh_hi, dh - dh_hi], axis=1).astype(BF16)
        return tuple(sums), tuple(value[0] for value in da)

    none = jnp.zeros((chans, rows), F32)
    sums, _ = lax.fori_loop(0, parts // chunk, deliver, ((none,) * 9, (none,) * 3))
    lane2 = lane[0]
    own_sums = jnp.zeros((chans, rows), F32)
    for n in range(9):
        own_sums = jnp.where(lane2 == n, jnp.sum(sums[n], axis=1, keepdims=True), own_sums)
    sums_hi = own_sums.astype(BF16).astype(F32)
    tail = jnp.concatenate([sums_hi, own_sums - sums_hi], axis=0).astype(BF16)
    send2[:, 48:64, :] = jnp.broadcast_to(tail[None], (parts, 16, rows))

    own2 = pltpu.make_async_copy(send2.at[me], recv2.at[me], recv_sem2)
    own2.start()

    def post2(peer):
        pltpu.make_async_remote_copy(
            src_ref=send2.at[peer], dst_ref=recv2.at[me], send_sem=send_sem2, recv_sem=recv_sem2, **target(peer)
        ).start()

    peers(post2)
    pltpu.make_async_copy(recv2, recv2, recv_sem2).wait()

    def back(value):
        return jnp.transpose(value.reshape(width, rows))

    pair = recv2[:, 0:16, :].astype(F32)
    mixed_ref[...] = back(pair[:, 0:8]).astype(BF16)
    gq_ref[...] = back(pair[:, 8:16]).astype(BF16)
    pair = recv2[:, 16:32, :].astype(F32)
    gk_ref[...] = back(pair[:, 0:8]).astype(BF16)
    gv_ref[...] = back(pair[:, 8:16]).astype(BF16)
    pair = recv2[:, 32:48, :].astype(F32)
    gh_ref[...] = back(pair[:, 0:8] + pair[:, 8:16])
    pair = recv2[:, 48:64, :].astype(F32)
    gtaps_ref[...] = back(pair[:, 0:8] + pair[:, 8:16])[0:9]

    sent = pl.ds(0, parts - 1)
    pltpu.make_async_copy(send.at[sent], send.at[sent], send_sem).wait()
    pltpu.make_async_copy(send2.at[sent], send2.at[sent], send_sem2).wait()


def local(q_proj, k_proj, v_proj, short_taps, long_filter, grad_out):
    parts = lax.axis_size("ctx")
    rows, width = q_proj.shape
    chans = width // parts
    tables = [jnp.asarray(t) for t in make_tables(parts, rows)]
    vmem = pl.BlockSpec(memory_space=pltpu.VMEM)
    like = jax.ShapeDtypeStruct((rows, width), BF16)
    outs = pl.pallas_call(
        kernel,
        out_shape=(
            like, like, like, like,
            jax.ShapeDtypeStruct((9, width), F32),
            jax.ShapeDtypeStruct((rows, width), F32),
        ),
        in_specs=[vmem] * 11,
        out_specs=(vmem,) * 6,
        scratch_shapes=[
            pltpu.VMEM((parts, 48, rows), BF16),
            pltpu.VMEM((parts, 48, rows), BF16),
            pltpu.VMEM((parts, 64, rows), BF16),
            pltpu.VMEM((parts, 64, rows), BF16),
            pltpu.VMEM((width, rows), F32),
            pltpu.VMEM((4, parts + 1, chans, rows), F32),
            pltpu.VMEM((3, parts, chans, rows), F32),
            pltpu.VMEM((3, parts, chans, rows), F32),
            pltpu.VMEM((3, width, 2 * rows), F32),
            pltpu.VMEM((3, parts, chans, rows), F32),
            pltpu.VMEM((width, 6 * rows), BF16),
            pltpu.SemaphoreType.DMA,
            pltpu.SemaphoreType.DMA,
            pltpu.SemaphoreType.DMA,
            pltpu.SemaphoreType.DMA,
        ],
        compiler_params=pltpu.CompilerParams(
            collective_id=0, has_side_effects=True, vmem_limit_bytes=40 << 20
        ),
        name="long_conv",
    )(q_proj, k_proj, v_proj, grad_out, long_filter, short_taps.reshape(9, width), *tables)
    mixed, gq, gk, gv, gtaps, gh = outs
    return mixed, gq, gk, gv, gtaps.reshape(3, 3, width), gh


def solution(mesh):
    field = P("ctx", "tp")
    taps = P(None, None, "tp")
    return jax.shard_map(
        local,
        mesh=mesh,
        in_specs=(field, field, field, taps, field, field),
        out_specs=(field, field, field, field, taps, field),
        check_vma=False,
    )
```

time: 680 us -> 90.1 us (0.13)
  the two profiles are of different devices: /device:TPU:64 before, /device:TPU:8 now
where the time goes in v1:
time: 90.1 us; the launch traced here: 89.6 us
  Pallas kernels  76.2 us (85%)
  local copies, waits for them, and re-layouts  12.6 us (14%)
    pallas_call x1, Pallas kernels, local(): pl.pallas_call(kernel, out_shape=(like, like, like, like, jax.ShapeDtypeS...  76.2 us
    unnamed x25, local copies, waits for them, and re-layouts  11.3 us

profile of v1, /device:TPU:8, one launch (start us, length us, event | category | flops | bytes accessed | tf_op | source)
XLA Modules:
  0.0 89.6 jit_solution(15489399659652115533)
XLA Ops:
  0.6 0.0 copy-start.7
  0.6 0.8 reshape.18.taps_ref
  1.4 0.0 copy-done.7
  1.4 0.0 copy-start
  1.4 1.0 %copy-done = bf16[768,256]{1,0:T(8,128)(2,1)S(1)} copy-done((bf16[768,256]{1,0:T(8,128)(2,1)S(1)}, bf16[768,256]{1,0:T(8,128)(2,1)}, u32[]{:S(2)}) %copy-start) | copy-done | bytes 393240
  2.4 0.0 copy-start.1
  2.4 0.9 %copy-done.1 = f32[128,512]{1,0:T(8,128)S(1)} copy-done((f32[128,512]{1,0:T(8,128)S(1)}, f32[128,512]{1,0:T(8,128)}, u32[]{:S(2)}) %copy-start.1) | copy-done | bytes 262168
  3.4 0.0 copy-start.2
  3.4 0.9 %copy-done.2 = bf16[128,512]{1,0:T(8,128)(2,1)S(1)} copy-done((bf16[128,512]{1,0:T(8,128)(2,1)S(1)}, bf16[128,512]{1,0:T(8,128)(2,1)}, u32[]{:S(2)}) %copy-start.2) | copy-done | bytes 131096
  4.3 0.0 copy-start.3
  4.3 0.9 %copy-done.3 = bf16[128,512]{1,0:T(8,128)(2,1)S(1)} copy-done((bf16[128,512]{1,0:T(8,128)(2,1)S(1)}, bf16[128,512]{1,0:T(8,128)(2,1)}, u32[]{:S(2)}) %copy-start.3) | copy-done | bytes 131096
  5.2 0.0 copy-start.4
  5.2 0.9 %copy-done.4 = bf16[128,512]{1,0:T(8,128)(2,1)S(1)} copy-done((bf16[128,512]{1,0:T(8,128)(2,1)S(1)}, bf16[128,512]{1,0:T(8,128)(2,1)}, u32[]{:S(2)}) %copy-start.4) | copy-done | bytes 131096
  6.1 0.0 copy-start.5
  6.1 0.9 %copy-done.5 = bf16[128,512]{1,0:T(8,128)(2,1)S(1)} copy-done((bf16[128,512]{1,0:T(8,128)(2,1)S(1)}, bf16[128,512]{1,0:T(8,128)(2,1)}, u32[]{:S(2)}) %copy-start.5) | copy-done | bytes 131096
  7.0 0.0 copy-start.6
  7.0 0.8 copy-done.6
  7.8 0.0 copy-start.8
  7.8 0.8 copy-done.8
  8.6 0.0 copy-start.9
  8.6 0.8 copy-done.9
  9.4 76.2 %long_conv.1 = (bf16[128,512]{1,0:T(8,128)(2,1)S(1)}, bf16[128,512]{1,0:T(8,128)(2,1)S(1)}, bf16[128,512]{1,0:T(8,128)(2,1)S(1)}, bf16[128,512]{1,0:T(8,128)(2,1...) custom-call(bf16[128,512]{1,0:T(8,128)(2,1)S(1)} %copy-done.2, bf16[128,512]{1,0:T(8,128)(2,1)S(1)} %copy-done.3, ...), custom_call_target="tpu_custom_call" | custom-call | tf_op jit(solution)/shard_map/long_conv/pallas_call | solution.py:264
  85.6 0.6 reshape.19
  86.2 0.7 copy.22
  86.9 0.7 copy.23
  87.5 0.7 copy.24
  88.2 0.7 copy.25
  88.9 0.7 copy.26
Async XLA Ops:
  0.6 0.8 copy-start.7
  1.4 1.0 %copy-start = (bf16[768,256]{1,0:T(8,128)(2,1)S(1)}, bf16[768,256]{1,0:T(8,128)(2,1)}, u32[]{:S(2)}) copy-start(bf16[768,256]{1,0:T(8,128)(2,1)} %constant.11.clone.second_ref) | copy-start | bytes 1179652
  2.4 0.9 %copy-start.1 = (f32[128,512]{1,0:T(8,128)S(1)}, f32[128,512]{1,0:T(8,128)}, u32[]{:S(2)}) copy-start(f32[128,512]{1,0:T(8,128)} %h_ref.1) | copy-start | bytes 786436
  3.4 0.9 %copy-start.2 = (bf16[128,512]{1,0:T(8,128)(2,1)S(1)}, bf16[128,512]{1,0:T(8,128)(2,1)}, u32[]{:S(2)}) copy-start(bf16[128,512]{1,0:T(8,128)(2,1)} %q_ref.1) | copy-start | bytes 393220
  4.3 0.9 %copy-start.3 = (bf16[128,512]{1,0:T(8,128)(2,1)S(1)}, bf16[128,512]{1,0:T(8,128)(2,1)}, u32[]{:S(2)}) copy-start(bf16[128,512]{1,0:T(8,128)(2,1)} %k_ref.1) | copy-start | bytes 393220
  5.2 0.9 %copy-start.4 = (bf16[128,512]{1,0:T(8,128)(2,1)S(1)}, bf16[128,512]{1,0:T(8,128)(2,1)}, u32[]{:S(2)}) copy-start(bf16[128,512]{1,0:T(8,128)(2,1)} %v_ref.1) | copy-start | bytes 393220
  6.1 0.9 %copy-start.5 = (bf16[128,512]{1,0:T(8,128)(2,1)S(1)}, bf16[128,512]{1,0:T(8,128)(2,1)}, u32[]{:S(2)}) copy-start(bf16[128,512]{1,0:T(8,128)(2,1)} %g_ref.1) | copy-start | bytes 393220
  7.0 0.8 copy-start.6
  7.8 0.8 copy-start.8
  8.6 0.8 copy-start.9

commit v2 on v1

--- a/solution.py
+++ b/solution.py
@@ -10,6 +10,23 @@
 
 F32 = jnp.float32
 BF16 = jnp.bfloat16
+SLOTS = 16
+RANGE = 32768.0
+TINY = 1e-30
+
+
+def encode(value):
+    power = value * value
+    power = power * power
+    power = power * power
+    return jnp.where(value < 0.0, -power, power)
+
+
+def decode(coded):
+    size = jnp.abs(coded)
+    fourth = lax.rsqrt(lax.rsqrt(size))
+    eighth = fourth * lax.rsqrt(fourth)
+    return jnp.where(coded < 0.0, -eighth, jnp.where(size > 0.0, eighth, 0.0))
 
 
 def split_table(table):
@@ -42,29 +59,49 @@
     return hi, (value - hi.astype(F32)).astype(BF16)
 
 
-def kernel(
-    q_ref, k_ref, v_ref, g_ref, h_ref, taps_ref, first_ref, second_ref, last_ref, cos_ref, sin_ref,
-    mixed_ref, gq_ref, gk_ref, gv_ref, gtaps_ref, gh_ref,
-    send, recv, send2, recv2, taps_t, x, feat, fields, spec, conv, lhs,
-    send_sem, recv_sem, send_sem2, recv_sem2,
+def sequence_kernel(
+    q_hbm, k_hbm, v_hbm, g_hbm, h_hbm, taps_hbm, first_hbm, second_hbm, last_hbm, cos_hbm, sin_hbm,
+    recv2, notes,
+    send, recv, send2, notes_out, taps_t, x, feat, fields, spec, conv, lhs,
+    send_sem, recv_sem, send_sem2, recv_sem2, note_send_sem, note_recv_sem,
+    q_ref, k_ref, v_ref, g_ref, h_ref, taps_ref, first_ref, second_ref, last_ref, cos_ref, sin_ref, load_sem,
 ):
     parts, chans, rows = 64, 8, 128
     width = parts * chans
     me = lax.axis_index("ctx")
     tp = lax.axis_index("tp")
     barrier = pltpu.get_barrier_semaphore()
+    loads = [
+        pltpu.make_async_copy(source, held, load_sem.at[n])
+        for n, (source, held) in enumerate((
+            (q_hbm, q_ref), (k_hbm, k_ref), (v_hbm, v_ref), (g_hbm, g_ref), (h_hbm, h_ref), (taps_hbm, taps_ref),
+            (first_hbm, first_ref), (second_hbm, second_ref), (last_hbm, last_ref), (cos_hbm, cos_ref), (sin_hbm, sin_ref),
+        ))
+    ]
+    for load in loads:
+        load.start()
 
     def peers(body):
         def step(i, carry):
-            body(jnp.bitwise_xor(me, i))
+            xi, zi = i & 3, (i >> 2) & 7
+            x_off = 2 + jnp.where((xi & 1) == 1, -((xi + 1) >> 1), xi >> 1)
+            z_off = 4 + jnp.where((zi & 1) == 1, -((zi + 1) >> 1), zi >> 1)
+            y_off = 1 - (i >> 5)
+            x_to = ((me >> 4) + x_off) & 3
+            y_to = ((me >> 3) & 1) ^ y_off
+            z_to = (me + z_off) & 7
+            body((x_to << 4) | (y_to << 3) | z_to)
             return carry
 
-        lax.fori_loop(1, parts, step, 0)
+        lax.fori_loop(0, parts - 1, step, 0)
 
     def target(peer):
         return dict(device_id=(peer, tp), device_id_type=pl.DeviceIdType.MESH)
 
     peers(lambda peer: pl.semaphore_signal(barrier, inc=1, **target(peer)))
+
+    for load in loads[:6]:
+        load.wait()
 
     def turned(ref):
         return jnp.transpose(ref[...].astype(F32)).reshape(parts, chans, rows)
@@ -74,7 +111,7 @@
     filt = turned(h_ref)
     filt_hi = filt.astype(BF16).astype(F32)
     send[:, 32:48, :] = jnp.concatenate([filt_hi, filt - filt_hi], axis=1).astype(BF16)
-    taps = jnp.concatenate([taps_ref[...], jnp.zeros((rows - 9, width), F32)], axis=0)
+    taps = jnp.concatenate([taps_ref[0], taps_ref[1], taps_ref[2], jnp.zeros((rows - 9, width), F32)], axis=0)
     taps_t[...] = jnp.transpose(taps)
 
     pl.semaphore_wait(barrier, parts - 1)
@@ -141,6 +178,8 @@
 
     lax.fori_loop(0, parts // chunk, featurize, 0)
 
+    for load in loads[6:]:
+        load.wait()
     turn_re, turn_im = cos_ref[...], sin_ref[...]
     first, second, last = first_ref[...], second_ref[...], last_ref[...]
     flat_fields = fields.reshape(3 * width, rows)
@@ -188,70 +227,143 @@
 
     lax.fori_loop(0, 3, inverse, 0)
 
-    def deliver(i, carry):
-        sums, edge = carry
-        p0 = (parts // chunk - 1 - i) * chunk
+    peak = []
+    for o in range(3):
+        top = jnp.max(jnp.max(jnp.abs(conv[o]), axis=0), axis=1, keepdims=True)
+        peak.append(jnp.broadcast_to(jnp.maximum(top, TINY), (chans, rows)))
+    gain = [RANGE / top for top in peak]
+    group = lax.broadcasted_iota(jnp.int32, (1, chans, rows), 2) // SLOTS
+    sublane = lax.broadcasted_iota(jnp.int32, (1, chans, rows), 1)
+
+    def flattened(value):
+        for shift in (SLOTS, 2 * SLOTS, 4 * SLOTS):
+            value = value + rolled(value, shift)
+        return jnp.sum(jnp.where(group == sublane, value, 0.0), axis=1, keepdims=True)
+
+    def placed(values, lane0):
+        out = jnp.zeros_like(values[0])
+        for n, value in enumerate(values):
+            at = lane0 + 2 * n
+            out = jnp.where((lane >= at) & (lane < at + 2), rolled(value, at) if at else value, out)
+        return out
+
+    def deliver(i, sums):
+        p0 = i * chunk
         here = pl.ds(p0, chunk)
+        there = pl.ds(p0 + 1, chunk)
         y, dz, dh = conv[0, here], conv[1, here], conv[2, here]
-        grad = x[3, pl.ds(p0 + 1, chunk)]
-        da = [dz * feat[2, here], grad * y, dz * feat[0, here]]
-        mixed = feat[1, here] * y
-        grads = []
+        a = [feat[s, here] for s in range(3)]
+        da = [dz * a[2], x[3, there] * y, dz * a[0]]
         sums = list(sums)
         for s in range(3):
-            value = jnp.concatenate([da[s], edge[s][None]], axis=0)
-            total = tap(s, 0) * da[s]
-            for j in (1, 2):
-                moved = rolled(value, -j)
-                total = total + tap(s, j) * jnp.where(lane >= rows - j, moved[1:], moved[:-1])
-            grads.append(total)
             d = delayed(s, p0)
             for j in range(3):
                 sums[3 * s + j] = sums[3 * s + j] + jnp.sum(da[s] * d[j], axis=0)
-        send2[here, 0:16, :] = jnp.concatenate([mixed, grads[0]], axis=1).astype(BF16)
-        send2[here, 16:32, :] = jnp.concatenate([grads[1], grads[2]], axis=1).astype(BF16)
-        dh_hi = dh.astype(BF16).astype(F32)
-        send2[here, 32:48, :] = jnp.concatenate([dh_hi, dh - dh_hi], axis=1).astype(BF16)
-        return tuple(sums), tuple(value[0] for value in da)
-
-    none = jnp.zeros((chans, rows), F32)
-    sums, _ = lax.fori_loop(0, parts // chunk, deliver, ((none,) * 9, (none,) * 3))
+        notes_out[here, 0:1, :] = flattened(placed(da, 9))
+        notes_out[there, 1:2, :] = flattened(placed(a, 0))
+        coded = [encode(value * gain[o][None]) for o, value in enumerate((y, dz, dh))]
+        send2[here, :, :] = jnp.concatenate(coded, axis=1).astype(BF16)
+        return tuple(sums)
+
+    sums = lax.fori_loop(0, parts // chunk, deliver, (jnp.zeros((chans, rows), F32),) * 9)
+    notes_out[parts, 0:1, :] = jnp.zeros((1, rows), F32)
     lane2 = lane[0]
-    own_sums = jnp.zeros((chans, rows), F32)
+    first_note = jnp.zeros((chans, rows), F32)
     for n in range(9):
-        own_sums = jnp.where(lane2 == n, jnp.sum(sums[n], axis=1, keepdims=True), own_sums)
-    sums_hi = own_sums.astype(BF16).astype(F32)
-    tail = jnp.concatenate([sums_hi, own_sums - sums_hi], axis=0).astype(BF16)
-    send2[:, 48:64, :] = jnp.broadcast_to(tail[None], (parts, 16, rows))
+        first_note = jnp.where(lane2 == n, jnp.sum(sums[n], axis=1, keepdims=True), first_note)
+    second_note = jnp.zeros((chans, rows), F32)
+    for o in range(3):
+        second_note = jnp.where(lane2 == 6 + o, peak[o], second_note)
+    both = jnp.concatenate([flattened(first_note[None]), flattened(second_note[None])], axis=1)
+    later = pl.ds(1, parts)
+    notes_out[later] = notes_out[later] + both
 
     own2 = pltpu.make_async_copy(send2.at[me], recv2.at[me], recv_sem2)
     own2.start()
+    own_note = pltpu.make_async_copy(notes_out.at[me + 1], notes.at[me], note_recv_sem)
+    own_note.start()
 
     def post2(peer):
         pltpu.make_async_remote_copy(
             src_ref=send2.at[peer], dst_ref=recv2.at[me], send_sem=send_sem2, recv_sem=recv_sem2, **target(peer)
         ).start()
+        pltpu.make_async_remote_copy(
+            src_ref=notes_out.at[peer + 1], dst_ref=notes.at[me], send_sem=note_send_sem, recv_sem=note_recv_sem, **target(peer)
+        ).start()
 
     peers(post2)
     pltpu.make_async_copy(recv2, recv2, recv_sem2).wait()
-
-    def back(value):
-        return jnp.transpose(value.reshape(width, rows))
-
-    pair = recv2[:, 0:16, :].astype(F32)
-    mixed_ref[...] = back(pair[:, 0:8]).astype(BF16)
-    gq_ref[...] = back(pair[:, 8:16]).astype(BF16)
-    pair = recv2[:, 16:32, :].astype(F32)
-    gk_ref[...] = back(pair[:, 0:8]).astype(BF16)
-    gv_ref[...] = back(pair[:, 8:16]).astype(BF16)
-    pair = recv2[:, 32:48, :].astype(F32)
-    gh_ref[...] = back(pair[:, 0:8] + pair[:, 8:16])
-    pair = recv2[:, 48:64, :].astype(F32)
-    gtaps_ref[...] = back(pair[:, 0:8] + pair[:, 8:16])[0:9]
-
+    pltpu.make_async_copy(notes, notes, note_recv_sem).wait()
     sent = pl.ds(0, parts - 1)
     pltpu.make_async_copy(send.at[sent], send.at[sent], send_sem).wait()
     pltpu.make_async_copy(send2.at[sent], send2.at[sent], send_sem2).wait()
+    pltpu.make_async_copy(notes_out.at[sent], notes_out.at[sent], note_send_sem).wait()
+
+
+def home_kernel(
+    q_hbm, k_hbm, v_hbm, g_hbm, taps_hbm, conv_hbm, notes_hbm,
+    mixed_hbm, gq_hbm, gk_hbm, gv_hbm, gtaps_hbm, gh_hbm,
+    q_ref, k_ref, v_ref, g_ref, taps_ref, conv_ref, notes_ref, load_sem,
+    mixed_ref, gq_ref, gk_ref, gv_ref, gtaps_ref, gh_ref, store_sem,
+    notes_t,
+):
+    parts, chans, rows = 64, 8, 128
+    loads = [
+        pltpu.make_async_copy(source, held, load_sem.at[n])
+        for n, (source, held) in enumerate((
+            (notes_hbm, notes_ref), (conv_hbm, conv_ref), (taps_hbm, taps_ref),
+            (q_hbm, q_ref), (k_hbm, k_ref), (v_hbm, v_ref), (g_hbm, g_ref),
+        ))
+    ]
+    for load in loads:
+        load.start()
+    stores = [
+        pltpu.make_async_copy(held, result, store_sem.at[n])
+        for n, (held, result) in enumerate((
+            (gtaps_ref, gtaps_hbm), (gh_ref, gh_hbm), (mixed_ref, mixed_hbm), (gq_ref, gq_hbm), (gk_ref, gk_hbm), (gv_ref, gv_hbm),
+        ))
+    ]
+    loads[0].wait()
+    for r in range(2):
+        note = notes_ref[:, r, :]
+        for c in range(chans):
+            notes_t[r, pl.ds(c, parts, stride=chans), :] = pltpu.roll(note, (rows - SLOTS * c) % rows, axis=1) if c else note
+    for load in loads[1:]:
+        load.wait()
+    row = lax.broadcasted_iota(jnp.int32, (rows, rows), 0)
+    inputs = (q_ref, k_ref, v_ref)
+    outputs = (gq_ref, gk_ref, gv_ref)
+    pad = jnp.zeros((8, rows), F32)
+    for b in range(4):
+        cols = slice(b * rows, (b + 1) * rows)
+        groups = slice(b * 16, (b + 1) * 16)
+        note = [jnp.transpose(notes_t[r, cols, :])[0:16] for r in range(2)]
+        for s in range(3):
+            gtaps_ref[s, :, cols] = note[0][3 * s : 3 * s + 3]
+        wide = decode(conv_ref[groups].astype(F32))
+        y, dz, dh = [
+            jnp.transpose(wide[:, 8 * o : 8 * o + 8].reshape(rows, rows)) * (note[1][6 + o : 7 + o] * (1.0 / RANGE))
+            for o in range(3)
+        ]
+        gh_ref[:, cols] = dh
+        tap = [[taps_ref[s, j : j + 1, cols] for j in range(3)] for s in range(3)]
+        a = []
+        for s in range(3):
+            value = inputs[s][:, cols].astype(F32)
+            joined = jnp.concatenate([pad, value], axis=0)
+            total = tap[s][0] * value + tap[s][1] * joined[7 : 7 + rows] + tap[s][2] * joined[6 : 6 + rows]
+            total = jnp.where(row == 0, note[1][2 * s : 2 * s + 1], total)
+            a.append(jnp.where(row == 1, note[1][2 * s + 1 : 2 * s + 2], total))
+        mixed_ref[:, cols] = (a[1] * y).astype(BF16)
+        da = [dz * a[2], g_ref[:, cols].astype(F32) * y, dz * a[0]]
+        for s in range(3):
+            joined = jnp.concatenate([da[s], note[0][9 + 2 * s : 11 + 2 * s], pad[0:6]], axis=0)
+            total = tap[s][0] * da[s] + tap[s][1] * joined[1 : 1 + rows] + tap[s][2] * joined[2 : 2 + rows]
+            outputs[s][:, cols] = total.astype(BF16)
+    for store in stores:
+        store.start()
+    for store in stores:
+        store.wait()
 
 
 def local(q_proj, k_proj, v_proj, short_taps, long_filter, grad_out):
@@ -259,22 +371,22 @@
     rows, width = q_proj.shape
     chans = width // parts
     tables = [jnp.asarray(t) for t in make_tables(parts, rows)]
-    vmem = pl.BlockSpec(memory_space=pltpu.VMEM)
-    like = jax.ShapeDtypeStruct((rows, width), BF16)
-    outs = pl.pallas_call(
-        kernel,
-        out_shape=(
-            like, like, like, like,
-            jax.ShapeDtypeStruct((9, width), F32),
-            jax.ShapeDtypeStruct((rows, width), F32),
-        ),
-        in_specs=[vmem] * 11,
-        out_specs=(vmem,) * 6,
+    hbm = pl.BlockSpec(memory_space=pltpu.HBM)
+    field = [pltpu.VMEM((rows, width), BF16) for _ in range(4)]
+    wide = [pltpu.VMEM((rows, width), F32)]
+    taps = [pltpu.VMEM((3, 3, width), F32)]
+    conv = jax.ShapeDtypeStruct((parts, 3 * chans, rows), BF16)
+    notes = jax.ShapeDtypeStruct((parts, 2, rows), F32)
+    conv, notes = pl.pallas_call(
+        sequence_kernel,
+        out_shape=(conv, notes),
+        in_specs=[hbm] * 11,
+        out_specs=(hbm, hbm),
         scratch_shapes=[
             pltpu.VMEM((parts, 48, rows), BF16),
             pltpu.VMEM((parts, 48, rows), BF16),
-            pltpu.VMEM((parts, 64, rows), BF16),
-            pltpu.VMEM((parts, 64, rows), BF16),
+            pltpu.VMEM((parts, 3 * chans, rows), BF16),
+            pltpu.VMEM((parts + 1, 2, rows), F32),
             pltpu.VMEM((width, rows), F32),
             pltpu.VMEM((4, parts + 1, chans, rows), F32),
             pltpu.VMEM((3, parts, chans, rows), F32),
@@ -282,18 +394,44 @@
             pltpu.VMEM((3, width, 2 * rows), F32),
             pltpu.VMEM((3, parts, chans, rows), F32),
             pltpu.VMEM((width, 6 * rows), BF16),
-            pltpu.SemaphoreType.DMA,
-            pltpu.SemaphoreType.DMA,
-            pltpu.SemaphoreType.DMA,
-            pltpu.SemaphoreType.DMA,
+            *[pltpu.SemaphoreType.DMA] * 6,
+            *field,
+            *wide,
+            *taps,
+            *[pltpu.VMEM(t.shape, t.dtype) for t in tables],
+            pltpu.SemaphoreType.DMA((11,)),
         ],
         compiler_params=pltpu.CompilerParams(
-            collective_id=0, has_side_effects=True, vmem_limit_bytes=40 << 20
+            collective_id=0, has_side_effects=True, vmem_limit_bytes=63 << 20
         ),
-        name="long_conv",
-    )(q_proj, k_proj, v_proj, grad_out, long_filter, short_taps.reshape(9, width), *tables)
-    mixed, gq, gk, gv, gtaps, gh = outs
-    return mixed, gq, gk, gv, gtaps.reshape(3, 3, width), gh
+        name="sequence_part",
+    )(q_proj, k_proj, v_proj, grad_out, long_filter, short_taps, *tables)
+    like = jax.ShapeDtypeStruct((rows, width), BF16)
+    mixed, gq, gk, gv, gtaps, gh = pl.pallas_call(
+        home_kernel,
+        out_shape=(
+            like, like, like, like,
+            jax.ShapeDtypeStruct((3, 3, width), F32),
+            jax.ShapeDtypeStruct((rows, width), F32),
+        ),
+        in_specs=[hbm] * 7,
+        out_specs=(hbm,) * 6,
+        scratch_shapes=[
+            *field,
+            *taps,
+            pltpu.VMEM(conv.shape, conv.dtype),
+            pltpu.VMEM(notes.shape, notes.dtype),
+            pltpu.SemaphoreType.DMA((7,)),
+            *field,
+            *taps,
+            *wide,
+            pltpu.SemaphoreType.DMA((6,)),
+            pltpu.VMEM((2, width, rows), F32),
+        ],
+        compiler_params=pltpu.CompilerParams(vmem_limit_bytes=63 << 20),
+        name="home_part",
+    )(q_proj, k_proj, v_proj, grad_out, short_taps, conv, notes)
+    return mixed, gq, gk, gv, gtaps, gh
 
 
 def solution(mesh):

time: 90.1 us -> 68 us (0.75)
  the two profiles are of different devices: /device:TPU:8 before, /device:TPU:1 now
where the time goes in v2:
time: 68 us; the launch traced here: 67.8 us
  Pallas kernels  67.2 us (99%)
    pallas_call x1, Pallas kernels, local(): pl.pallas_call(sequence_kernel, out_shape=(conv, notes), in_specs=[hbm] *...  64 us
    pallas_call x1, Pallas kernels, local(): pl.pallas_call(home_kernel, out_shape=(like, like, like, like, jax.ShapeD...  3.15 us

profile of v2, /device:TPU:1, one launch (start us, length us, event | category | flops | bytes accessed | tf_op | source)
XLA Modules:
  0.0 67.8 jit_solution(8554488856121083052)
XLA Ops:
  0.6 64.0 %sequence_part.1 = (bf16[64,24,128]{2,1,0:T(8,128)(2,1)}, f32[64,2,128]{2,1,0:T(2,128)}) custom-call(bf16[128,512]{1,0:T(8,128)(2,1)} %q_hbm.3, bf16[128,512]{1,0:T(8,128)(2,1)} %k_hbm.3, bf16[128,512]{1,0:T(8,128)(2,1)} %v_hbm.3, bf16[128,512]{1,0:T(8,128)(2,1)} %g_hbm.3, f32[128,512]{1,0:T(8,128)} %h_hbm.1, f32[3,3,512]{2,1,0:T(4,128)} %taps_hbm.3, ...), custom_call_target="tpu_custom_call" | custom-call | tf_op jit(solution)/shard_map/sequence_part/pallas_call | solution.py:380
  64.7 3.1 %home_part.1 = (bf16[128,512]{1,0:T(8,128)(2,1)}, bf16[128,512]{1,0:T(8,128)(2,1)}, bf16[128,512]{1,0:T(8,128)(2,1)}, bf16[128,512]{1,0:T(8,128)(2,1)}, f32[3,3,512]{2,1,0:T(4,128)}, /*index=5*/f32[128,512]{1,0:T(8,128)}) custom-call(bf16[128,512]{1,0:T(8,128)(2,1)} %q_hbm.3, bf16[128,512]{1,0:T(8,128)(2,1)} %k_hbm.3, bf16[128,512]{1,0:T(8,128)(2,1)} %v_hbm.3, ...), custom_call_target="tpu_custom_call" | custom-call | tf_op jit(solution)/shard_map/home_part/pallas_call | solution.py:410

commit v3 on v2

--- a/solution.py
+++ b/solution.py
@@ -61,9 +61,9 @@
 
 def sequence_kernel(
     q_hbm, k_hbm, v_hbm, g_hbm, h_hbm, taps_hbm, first_hbm, second_hbm, last_hbm, cos_hbm, sin_hbm,
-    recv2, notes,
-    send, recv, send2, notes_out, taps_t, x, feat, fields, spec, conv, lhs,
-    send_sem, recv_sem, send_sem2, recv_sem2, note_send_sem, note_recv_sem,
+    y_in, d_in, notes,
+    wave1, wave2, peaks, got1, got2, got_peaks, y_out, d_out, notes_out, taps_t, x, feat, fields, spec, conv, lhs,
+    send_sem, recv_sem,
     q_ref, k_ref, v_ref, g_ref, h_ref, taps_ref, first_ref, second_ref, last_ref, cos_ref, sin_ref, load_sem,
 ):
     parts, chans, rows = 64, 8, 128
@@ -78,8 +78,6 @@
             (first_hbm, first_ref), (second_hbm, second_ref), (last_hbm, last_ref), (cos_hbm, cos_ref), (sin_hbm, sin_ref),
         ))
     ]
-    for load in loads:
-        load.start()
 
     def peers(body):
         def step(i, carry):
@@ -99,6 +97,8 @@
         return dict(device_id=(peer, tp), device_id_type=pl.DeviceIdType.MESH)
 
     peers(lambda peer: pl.semaphore_signal(barrier, inc=1, **target(peer)))
+    for load in loads:
+        load.start()
 
     for load in loads[:6]:
         load.wait()
@@ -106,25 +106,37 @@
     def turned(ref):
         return jnp.transpose(ref[...].astype(F32)).reshape(parts, chans, rows)
 
-    send[:, 0:16, :] = jnp.concatenate([turned(q_ref), turned(k_ref)], axis=1).astype(BF16)
-    send[:, 16:32, :] = jnp.concatenate([turned(v_ref), turned(g_ref)], axis=1).astype(BF16)
     filt = turned(h_ref)
-    filt_hi = filt.astype(BF16).astype(F32)
-    send[:, 32:48, :] = jnp.concatenate([filt_hi, filt - filt_hi], axis=1).astype(BF16)
+    peak = jnp.max(jnp.max(jnp.abs(filt), axis=2, keepdims=True), axis=1, keepdims=True)
+    peak = jnp.broadcast_to(jnp.maximum(peak, TINY), (parts, 1, rows))
+    peaks[...] = peak
+    wave1[...] = jnp.concatenate([turned(q_ref), turned(v_ref), encode(filt * (RANGE / peak))], axis=1).astype(BF16)
+    wave2[...] = jnp.concatenate([turned(k_ref), turned(g_ref)], axis=1).astype(BF16)
     taps = jnp.concatenate([taps_ref[0], taps_ref[1], taps_ref[2], jnp.zeros((rows - 9, width), F32)], axis=0)
     taps_t[...] = jnp.transpose(taps)
 
     pl.semaphore_wait(barrier, parts - 1)
-    own = pltpu.make_async_copy(send.at[me], recv.at[me], recv_sem)
-    own.start()
-
-    def post(peer):
-        pltpu.make_async_remote_copy(
-            src_ref=send.at[peer], dst_ref=recv.at[me], send_sem=send_sem, recv_sem=recv_sem, **target(peer)
-        ).start()
-
-    peers(post)
-    pltpu.make_async_copy(recv, recv, recv_sem).wait()
+
+    def exchange(moves):
+        for source, result, n, skip in moves:
+            pltpu.make_async_copy(source.at[me + skip], result.at[me], recv_sem.at[n]).start()
+
+        def post(peer):
+            for source, result, n, skip in moves:
+                pltpu.make_async_remote_copy(
+                    src_ref=source.at[peer + skip], dst_ref=result.at[me],
+                    send_sem=send_sem.at[n], recv_sem=recv_sem.at[n], **target(peer)
+                ).start()
+
+        peers(post)
+
+    def arrived(result, n):
+        pltpu.make_async_copy(result, result, recv_sem.at[n]).wait()
+
+    exchange([(wave1, got1, 0, 0), (peaks, got_peaks, 1, 0)])
+    exchange([(wave2, got2, 2, 0)])
+    arrived(got1, 0)
+    arrived(got_peaks, 1)
 
     own_taps = taps_t[pl.ds(pl.multiple_of(me * chans, chans), chans), :]
 
@@ -140,21 +152,25 @@
 
     x[:, 0] = jnp.zeros((4, chans, rows), F32)
 
-    def unpack(i, carry):
+    def unpack1(i, carry):
         p0 = i * chunk
         here = pl.ds(p0, chunk)
         there = pl.ds(p0 + 1, chunk)
-        qk = recv[here, 0:16, :].astype(F32)
-        vg = recv[here, 16:32, :].astype(F32)
-        hh = recv[here, 32:48, :].astype(F32)
-        x[0, there] = qk[:, 0:8]
-        x[1, there] = qk[:, 8:16]
-        x[2, there] = vg[:, 0:8]
-        x[3, there] = vg[:, 8:16]
-        fields[1, here] = hh[:, 0:8] + hh[:, 8:16]
-        return carry
-
-    lax.fori_loop(0, parts // chunk, unpack, 0)
+        block = got1[here].astype(F32)
+        x[0, there] = block[:, 0:8]
+        x[2, there] = block[:, 8:16]
+        fields[1, here] = decode(block[:, 16:24]) * (got_peaks[here] * (1.0 / RANGE))
+        return carry
+
+    def unpack2(i, carry):
+        p0 = i * chunk
+        there = pl.ds(p0 + 1, chunk)
+        block = got2[pl.ds(p0, chunk)].astype(F32)
+        x[1, there] = block[:, 0:8]
+        x[3, there] = block[:, 8:16]
+        return carry
+
+    lax.fori_loop(0, parts // chunk, unpack1, 0)
 
     def delayed(s, p0):
         value = x[s, pl.ds(p0, chunk + 1)]
@@ -164,19 +180,23 @@
             out.append(jnp.where(lane < j, moved[:-1], moved[1:]))
         return out
 
-    def featurize(i, carry):
+    def featured(s, p0):
+        d = delayed(s, p0)
+        value = tap(s, 0) * d[0] + tap(s, 1) * d[1] + tap(s, 2) * d[2]
+        feat[s, pl.ds(p0, chunk)] = value
+        return value
+
+    def featurize1(i, carry):
         p0 = i * chunk
-        here = pl.ds(p0, chunk)
-        a = []
-        for s in range(3):
-            d = delayed(s, p0)
-            a.append(tap(s, 0) * d[0] + tap(s, 1) * d[1] + tap(s, 2) * d[2])
-            feat[s, here] = a[s]
-        fields[0, here] = a[0] * a[2]
-        fields[2, here] = a[1] * x[3, pl.ds(p0 + 1, chunk)]
-        return carry
-
-    lax.fori_loop(0, parts // chunk, featurize, 0)
+        fields[0, pl.ds(p0, chunk)] = featured(0, p0) * featured(2, p0)
+        return carry
+
+    def featurize2(i, carry):
+        p0 = i * chunk
+        fields[2, pl.ds(p0, chunk)] = featured(1, p0) * x[3, pl.ds(p0 + 1, chunk)]
+        return carry
+
+    lax.fori_loop(0, parts // chunk, featurize1, 0)
 
     for load in loads[6:]:
         load.wait()
@@ -200,7 +220,7 @@
         spec[f] = jnp.dot(lhs[...], second, preferred_element_type=F32)
         return carry
 
-    lax.fori_loop(0, 3, forward, 0)
+    lax.fori_loop(0, 2, forward, 0)
 
     def inverse(o, carry):
         f_a = jnp.where(o == 0, 0, 2)
@@ -225,13 +245,30 @@
                 flat_conv[pl.ds(o * width + c + e, parts, stride=chans), :] = out[:, e * rows : (e + 1) * rows]
         return carry
 
-    lax.fori_loop(0, 3, inverse, 0)
-
-    peak = []
-    for o in range(3):
+    def scaled(o):
         top = jnp.max(jnp.max(jnp.abs(conv[o]), axis=0), axis=1, keepdims=True)
-        peak.append(jnp.broadcast_to(jnp.maximum(top, TINY), (chans, rows)))
-    gain = [RANGE / top for top in peak]
+        top = jnp.broadcast_to(jnp.maximum(top, TINY), (chans, rows))
+        return top, (RANGE / top)[None]
+
+    lax.fori_loop(0, 1, inverse, 0)
+    y_peak, y_gain = scaled(0)
+
+    def code_y(i, carry):
+        here = pl.ds(i * chunk, chunk)
+        y_out[here] = encode(conv[0, here] * y_gain).astype(BF16)
+        return carry
+
+    lax.fori_loop(0, parts // chunk, code_y, 0)
+    exchange([(y_out, y_in, 3, 0)])
+
+    arrived(got2, 2)
+    lax.fori_loop(0, parts // chunk, unpack2, 0)
+    lax.fori_loop(0, parts // chunk, featurize2, 0)
+    lax.fori_loop(2, 3, forward, 0)
+    lax.fori_loop(1, 3, inverse, 0)
+    dz_peak, dz_gain = scaled(1)
+    dh_peak, dh_gain = scaled(2)
+    peak = (y_peak, dz_peak, dh_peak)
     group = lax.broadcasted_iota(jnp.int32, (1, chans, rows), 2) // SLOTS
     sublane = lax.broadcasted_iota(jnp.int32, (1, chans, rows), 1)
 
@@ -261,8 +298,7 @@
                 sums[3 * s + j] = sums[3 * s + j] + jnp.sum(da[s] * d[j], axis=0)
         notes_out[here, 0:1, :] = flattened(placed(da, 9))
         notes_out[there, 1:2, :] = flattened(placed(a, 0))
-        coded = [encode(value * gain[o][None]) for o, value in enumerate((y, dz, dh))]
-        send2[here, :, :] = jnp.concatenate(coded, axis=1).astype(BF16)
+        d_out[here] = jnp.concatenate([encode(dz * dz_gain), encode(dh * dh_gain)], axis=1).astype(BF16)
         return tuple(sums)
 
     sums = lax.fori_loop(0, parts // chunk, deliver, (jnp.zeros((chans, rows), F32),) * 9)
@@ -278,32 +314,19 @@
     later = pl.ds(1, parts)
     notes_out[later] = notes_out[later] + both
 
-    own2 = pltpu.make_async_copy(send2.at[me], recv2.at[me], recv_sem2)
-    own2.start()
-    own_note = pltpu.make_async_copy(notes_out.at[me + 1], notes.at[me], note_recv_sem)
-    own_note.start()
-
-    def post2(peer):
-        pltpu.make_async_remote_copy(
-            src_ref=send2.at[peer], dst_ref=recv2.at[me], send_sem=send_sem2, recv_sem=recv_sem2, **target(peer)
-        ).start()
-        pltpu.make_async_remote_copy(
-            src_ref=notes_out.at[peer + 1], dst_ref=notes.at[me], send_sem=note_send_sem, recv_sem=note_recv_sem, **target(peer)
-        ).start()
-
-    peers(post2)
-    pltpu.make_async_copy(recv2, recv2, recv_sem2).wait()
-    pltpu.make_async_copy(notes, notes, note_recv_sem).wait()
-    sent = pl.ds(0, parts - 1)
-    pltpu.make_async_copy(send.at[sent], send.at[sent], send_sem).wait()
-    pltpu.make_async_copy(send2.at[sent], send2.at[sent], send_sem2).wait()
-    pltpu.make_async_copy(notes_out.at[sent], notes_out.at[sent], note_send_sem).wait()
+    exchange([(d_out, d_in, 4, 0), (notes_out, notes, 5, 1)])
+    arrived(y_in, 3)
+    arrived(d_in, 4)
+    arrived(notes, 5)
+    for n, source in enumerate((wave1, peaks, wave2, y_out, d_out, notes_out)):
+        sent = source.at[pl.ds(0, parts - 1)]
+        pltpu.make_async_copy(sent, sent, send_sem.at[n]).wait()
 
 
 def home_kernel(
-    q_hbm, k_hbm, v_hbm, g_hbm, taps_hbm, conv_hbm, notes_hbm,
+    q_hbm, k_hbm, v_hbm, g_hbm, taps_hbm, y_hbm, d_hbm, notes_hbm,
     mixed_hbm, gq_hbm, gk_hbm, gv_hbm, gtaps_hbm, gh_hbm,
-    q_ref, k_ref, v_ref, g_ref, taps_ref, conv_ref, notes_ref, load_sem,
+    q_ref, k_ref, v_ref, g_ref, taps_ref, y_ref, d_ref, notes_ref, load_sem,
     mixed_ref, gq_ref, gk_ref, gv_ref, gtaps_ref, gh_ref, store_sem,
     notes_t,
 ):
@@ -311,7 +334,7 @@
     loads = [
         pltpu.make_async_copy(source, held, load_sem.at[n])
         for n, (source, held) in enumerate((
-            (notes_hbm, notes_ref), (conv_hbm, conv_ref), (taps_hbm, taps_ref),
+            (notes_hbm, notes_ref), (y_hbm, y_ref), (d_hbm, d_ref), (taps_hbm, taps_ref),
             (q_hbm, q_ref), (k_hbm, k_ref), (v_hbm, v_ref), (g_hbm, g_ref),
         ))
     ]
@@ -340,10 +363,10 @@
         note = [jnp.transpose(notes_t[r, cols, :])[0:16] for r in range(2)]
         for s in range(3):
             gtaps_ref[s, :, cols] = note[0][3 * s : 3 * s + 3]
-        wide = decode(conv_ref[groups].astype(F32))
+        pair = decode(d_ref[groups].astype(F32))
         y, dz, dh = [
-            jnp.transpose(wide[:, 8 * o : 8 * o + 8].reshape(rows, rows)) * (note[1][6 + o : 7 + o] * (1.0 / RANGE))
-            for o in range(3)
+            jnp.transpose(value.reshape(rows, rows)) * (note[1][6 + o : 7 + o] * (1.0 / RANGE))
+            for o, value in enumerate((decode(y_ref[groups].astype(F32)), pair[:, 0:8], pair[:, 8:16]))
         ]
         gh_ref[:, cols] = dh
         tap = [[taps_ref[s, j : j + 1, cols] for j in range(3)] for s in range(3)]
@@ -375,17 +398,22 @@
     field = [pltpu.VMEM((rows, width), BF16) for _ in range(4)]
     wide = [pltpu.VMEM((rows, width), F32)]
     taps = [pltpu.VMEM((3, 3, width), F32)]
-    conv = jax.ShapeDtypeStruct((parts, 3 * chans, rows), BF16)
+    y_all = jax.ShapeDtypeStruct((parts, chans, rows), BF16)
+    d_all = jax.ShapeDtypeStruct((parts, 2 * chans, rows), BF16)
     notes = jax.ShapeDtypeStruct((parts, 2, rows), F32)
-    conv, notes = pl.pallas_call(
+    back = pl.pallas_call(
         sequence_kernel,
-        out_shape=(conv, notes),
+        out_shape=(y_all, d_all, notes),
         in_specs=[hbm] * 11,
-        out_specs=(hbm, hbm),
+        out_specs=(hbm,) * 3,
         scratch_shapes=[
-            pltpu.VMEM((parts, 48, rows), BF16),
-            pltpu.VMEM((parts, 48, rows), BF16),
-            pltpu.VMEM((parts, 3 * chans, rows), BF16),
+            *[
+                pltpu.VMEM((parts, 3 * chans, rows), BF16),
+                pltpu.VMEM((parts, 2 * chans, rows), BF16),
+                pltpu.VMEM((parts, 1, rows), F32),
+            ] * 2,
+            pltpu.VMEM(y_all.shape, BF16),
+            pltpu.VMEM(d_all.shape, BF16),
             pltpu.VMEM((parts + 1, 2, rows), F32),
             pltpu.VMEM((width, rows), F32),
             pltpu.VMEM((4, parts + 1, chans, rows), F32),
@@ -394,7 +422,7 @@
             pltpu.VMEM((3, width, 2 * rows), F32),
             pltpu.VMEM((3, parts, chans, rows), F32),
             pltpu.VMEM((width, 6 * rows), BF16),
-            *[pltpu.SemaphoreType.DMA] * 6,
+            *[pltpu.SemaphoreType.DMA((6,))] * 2,
             *field,
             *wide,
             *taps,
@@ -414,14 +442,13 @@
             jax.ShapeDtypeStruct((3, 3, width), F32),
             jax.ShapeDtypeStruct((rows, width), F32),
         ),
-        in_specs=[hbm] * 7,
+        in_specs=[hbm] * 8,
         out_specs=(hbm,) * 6,
         scratch_shapes=[
             *field,
             *taps,
-            pltpu.VMEM(conv.shape, conv.dtype),
-            pltpu.VMEM(notes.shape, notes.dtype),
-            pltpu.SemaphoreType.DMA((7,)),
+            *[pltpu.VMEM(value.shape, value.dtype) for value in back],
+            pltpu.SemaphoreType.DMA((8,)),
             *field,
             *taps,
             *wide,
@@ -430,7 +457,7 @@
         ],
         compiler_params=pltpu.CompilerParams(vmem_limit_bytes=63 << 20),
         name="home_part",
-    )(q_proj, k_proj, v_proj, grad_out, short_taps, conv, notes)
+    )(q_proj, k_proj, v_proj, grad_out, short_taps, *back)
     return mixed, gq, gk, gv, gtaps, gh
 
 

time: 68 us -> 58.3 us (0.86)
  the two profiles are of different devices: /device:TPU:1 before, /device:TPU:8 now
where the time goes in v3:
time: 58.3 us; the launch traced here: 58.1 us
  Pallas kernels  57.5 us (99%)
  between operations  0.64 us (1%)
    pallas_call x1, Pallas kernels, local(): pl.pallas_call(sequence_kernel, out_shape=(y_all, d_all, notes), in_specs...  54.3 us
    pallas_call x1, Pallas kernels, local(): pl.pallas_call(home_kernel, out_shape=(like, like, like, like, jax.ShapeD...  3.18 us

profile of v3, /device:TPU:8, one launch (start us, length us, event | category | flops | bytes accessed | tf_op | source)
XLA Modules:
  0.0 58.1 jit_solution(4136559144759459556)
XLA Ops:
  0.6 54.3 %sequence_part.1 = (bf16[64,8,128]{2,1,0:T(8,128)(2,1)}, bf16[64,16,128]{2,1,0:T(8,128)(2,1)}, f32[64,2,128]{2,1,0:T(2,128)}) custom-call(bf16[128,512]{1,0:T(8,128)(2,1)} %q_hbm.3, bf16[128,512]{1,0:T(8,128)(2,1)} %k_hbm.3, bf16[128,512]{1,0:T(8,128)(2,1)} %v_hbm.3, bf16[128,512]{1,0:T(8,128)(2,1)} %g_hbm.3, f32[128,512]{1,0:T(8,128)} %h_hbm.1, ...), custom_call_target="tpu_custom_call" | custom-call | tf_op jit(solution)/shard_map/sequence_part/pallas_call | solution.py:404
  55.0 3.2 %home_part.1 = (bf16[128,512]{1,0:T(8,128)(2,1)}, bf16[128,512]{1,0:T(8,128)(2,1)}, bf16[128,512]{1,0:T(8,128)(2,1)}, bf16[128,512]{1,0:T(8,128)(2,1)}, f32[3,3,512]{2,1,0:T(4,128)}, /*index=5*/f32[128,512]{1,0:T(8,128)}) custom-call(bf16[128,512]{1,0:T(8,128)(2,1)} %q_hbm.3, bf16[128,512]{1,0:T(8,128)(2,1)} %k_hbm.3, bf16[128,512]{1,0:T(8,128)(2,1)} %v_hbm.3, ...), custom_call_target="tpu_custom_call" | custom-call | tf_op jit(solution)/shard_map/home_part/pallas_call | solution.py:438

commit v4 on v3

--- a/solution.py
+++ b/solution.py
@@ -62,7 +62,7 @@
 def sequence_kernel(
     q_hbm, k_hbm, v_hbm, g_hbm, h_hbm, taps_hbm, first_hbm, second_hbm, last_hbm, cos_hbm, sin_hbm,
     y_in, d_in, notes,
-    wave1, wave2, peaks, got1, got2, got_peaks, y_out, d_out, notes_out, taps_t, x, feat, fields, spec, conv, lhs,
+    wave1, wave2, peaks, got1, got2, got_peaks, y_out, d_out, notes_out, taps_t, x, late, feat, fields, spec, conv, lhs,
     send_sem, recv_sem,
     q_ref, k_ref, v_ref, g_ref, h_ref, taps_ref, first_ref, second_ref, last_ref, cos_ref, sin_ref, load_sem,
 ):
@@ -81,10 +81,10 @@
 
     def peers(body):
         def step(i, carry):
-            xi, zi = i & 3, (i >> 2) & 7
+            xi, zi = (i >> 1) & 3, i >> 3
             x_off = 2 + jnp.where((xi & 1) == 1, -((xi + 1) >> 1), xi >> 1)
             z_off = 4 + jnp.where((zi & 1) == 1, -((zi + 1) >> 1), zi >> 1)
-            y_off = 1 - (i >> 5)
+            y_off = 1 - (i & 1)
             x_to = ((me >> 4) + x_off) & 3
             y_to = ((me >> 3) & 1) ^ y_off
             z_to = (me + z_off) & 7
@@ -170,7 +170,7 @@
         x[3, there] = block[:, 8:16]
         return carry
 
-    lax.fori_loop(0, parts // chunk, unpack1, 0)
+    lax.fori_loop(0, parts // chunk, unpack1, 0, unroll=True)
 
     def delayed(s, p0):
         value = x[s, pl.ds(p0, chunk + 1)]
@@ -182,8 +182,11 @@
 
     def featured(s, p0):
         d = delayed(s, p0)
+        here = pl.ds(p0, chunk)
+        late[s, 0, here] = d[1]
+        late[s, 1, here] = d[2]
         value = tap(s, 0) * d[0] + tap(s, 1) * d[1] + tap(s, 2) * d[2]
-        feat[s, pl.ds(p0, chunk)] = value
+        feat[s, here] = value
         return value
 
     def featurize1(i, carry):
@@ -196,7 +199,7 @@
         fields[2, pl.ds(p0, chunk)] = featured(1, p0) * x[3, pl.ds(p0 + 1, chunk)]
         return carry
 
-    lax.fori_loop(0, parts // chunk, featurize1, 0)
+    lax.fori_loop(0, parts // chunk, featurize1, 0, unroll=True)
 
     for load in loads[6:]:
         load.wait()
@@ -208,7 +211,7 @@
     def twiddled(re, im):
         return re * turn_re - im * turn_im, re * turn_im + im * turn_re
 
-    def forward(f, carry):
+    def forward(f):
         for c in range(0, chans, 2):
             pair = [flat_fields[pl.ds(f * width + c + e, parts, stride=chans), :] for e in (0, 1)]
             hi, lo = halves(jnp.concatenate(pair, axis=1))
@@ -216,24 +219,22 @@
             for e in (0, 1):
                 re, im = twiddled(mid[:parts, e * rows : (e + 1) * rows], mid[parts:, e * rows : (e + 1) * rows])
                 hi, lo = halves(jnp.concatenate([re, im], axis=1))
-                lhs[(c + e) * parts : (c + e + 1) * parts, :] = jnp.concatenate([hi, lo, hi], axis=1)
-        spec[f] = jnp.dot(lhs[...], second, preferred_element_type=F32)
-        return carry
-
-    lax.fori_loop(0, 2, forward, 0)
-
-    def inverse(o, carry):
-        f_a = jnp.where(o == 0, 0, 2)
-        f_b = jnp.where(o == 2, 0, 1)
-        sign = jnp.where(o == 0, 1.0, -1.0).astype(F32)
+                lhs[f, (c + e) * parts : (c + e + 1) * parts, :] = jnp.concatenate([hi, lo, hi], axis=1)
+        spec[f] = jnp.dot(lhs[f], second, preferred_element_type=F32)
+
+    forward(0)
+    forward(1)
+
+    def inverse(o):
+        f_a, f_b, sign = ((0, 1, 1.0), (2, 1, -1.0), (2, 0, -1.0))[o]
         for c in range(chans):
             block = pl.ds(c * parts, parts)
             a, b = spec[f_a, block, :], spec[f_b, block, :]
             a_re, a_im, b_re, b_im = a[:, :rows], a[:, rows:], b[:, :rows], sign * b[:, rows:]
             re, im = a_re * b_re - a_im * b_im, a_re * b_im + a_im * b_re
             hi, lo = halves(jnp.concatenate([re, -im], axis=1))
-            lhs[c * parts : (c + 1) * parts, :] = jnp.concatenate([hi, lo, hi], axis=1)
-        mid = jnp.dot(lhs[...], second, preferred_element_type=F32)
+            lhs[o, c * parts : (c + 1) * parts, :] = jnp.concatenate([hi, lo, hi], axis=1)
+        mid = jnp.dot(lhs[o], second, preferred_element_type=F32)
         for c in range(0, chans, 2):
             pair = []
             for e in (0, 1):
@@ -243,14 +244,13 @@
             out = jnp.dot(last, jnp.concatenate([hi, lo, hi], axis=0), preferred_element_type=F32)
             for e in (0, 1):
                 flat_conv[pl.ds(o * width + c + e, parts, stride=chans), :] = out[:, e * rows : (e + 1) * rows]
-        return carry
 
     def scaled(o):
         top = jnp.max(jnp.max(jnp.abs(conv[o]), axis=0), axis=1, keepdims=True)
         top = jnp.broadcast_to(jnp.maximum(top, TINY), (chans, rows))
         return top, (RANGE / top)[None]
 
-    lax.fori_loop(0, 1, inverse, 0)
+    inverse(0)
     y_peak, y_gain = scaled(0)
 
     def code_y(i, carry):
@@ -258,17 +258,28 @@
         y_out[here] = encode(conv[0, here] * y_gain).astype(BF16)
         return carry
 
-    lax.fori_loop(0, parts // chunk, code_y, 0)
+    lax.fori_loop(0, parts // chunk, code_y, 0, unroll=True)
     exchange([(y_out, y_in, 3, 0)])
 
     arrived(got2, 2)
-    lax.fori_loop(0, parts // chunk, unpack2, 0)
-    lax.fori_loop(0, parts // chunk, featurize2, 0)
-    lax.fori_loop(2, 3, forward, 0)
-    lax.fori_loop(1, 3, inverse, 0)
+    lax.fori_loop(0, parts // chunk, unpack2, 0, unroll=True)
+    lax.fori_loop(0, parts // chunk, featurize2, 0, unroll=True)
+    forward(2)
+    inverse(1)
+    inverse(2)
     dz_peak, dz_gain = scaled(1)
     dh_peak, dh_gain = scaled(2)
     peak = (y_peak, dz_peak, dh_peak)
+
+    def code_d(i, carry):
+        here = pl.ds(i * chunk, chunk)
+        pair = [encode(conv[1, here] * dz_gain), encode(conv[2, here] * dh_gain)]
+        d_out[here] = jnp.concatenate(pair, axis=1).astype(BF16)
+        return carry
+
+    lax.fori_loop(0, parts // chunk, code_d, 0, unroll=True)
+    exchange([(d_out, d_in, 4, 0)])
+
     group = lax.broadcasted_iota(jnp.int32, (1, chans, rows), 2) // SLOTS
     sublane = lax.broadcasted_iota(jnp.int32, (1, chans, rows), 1)
 
@@ -284,24 +295,23 @@
             out = jnp.where((lane >= at) & (lane < at + 2), rolled(value, at) if at else value, out)
         return out
 
-    def deliver(i, sums):
+    def tally(i, sums):
         p0 = i * chunk
         here = pl.ds(p0, chunk)
         there = pl.ds(p0 + 1, chunk)
-        y, dz, dh = conv[0, here], conv[1, here], conv[2, here]
+        y, dz = conv[0, here], conv[1, here]
         a = [feat[s, here] for s in range(3)]
         da = [dz * a[2], x[3, there] * y, dz * a[0]]
         sums = list(sums)
         for s in range(3):
-            d = delayed(s, p0)
+            d = (x[s, there], late[s, 0, here], late[s, 1, here])
             for j in range(3):
                 sums[3 * s + j] = sums[3 * s + j] + jnp.sum(da[s] * d[j], axis=0)
         notes_out[here, 0:1, :] = flattened(placed(da, 9))
         notes_out[there, 1:2, :] = flattened(placed(a, 0))
-        d_out[here] = jnp.concatenate([encode(dz * dz_gain), encode(dh * dh_gain)], axis=1).astype(BF16)
         return tuple(sums)
 
-    sums = lax.fori_loop(0, parts // chunk, deliver, (jnp.zeros((chans, rows), F32),) * 9)
+    sums = lax.fori_loop(0, parts // chunk, tally, (jnp.zeros((chans, rows), F32),) * 9, unroll=2)
     notes_out[parts, 0:1, :] = jnp.zeros((1, rows), F32)
     lane2 = lane[0]
     first_note = jnp.zeros((chans, rows), F32)
@@ -314,7 +324,7 @@
     later = pl.ds(1, parts)
     notes_out[later] = notes_out[later] + both
 
-    exchange([(d_out, d_in, 4, 0), (notes_out, notes, 5, 1)])
+    exchange([(notes_out, notes, 5, 1)])
     arrived(y_in, 3)
     arrived(d_in, 4)
     arrived(notes, 5)
@@ -340,12 +350,10 @@
     ]
     for load in loads:
         load.start()
-    stores = [
-        pltpu.make_async_copy(held, result, store_sem.at[n])
-        for n, (held, result) in enumerate((
-            (gtaps_ref, gtaps_hbm), (gh_ref, gh_hbm), (mixed_ref, mixed_hbm), (gq_ref, gq_hbm), (gk_ref, gk_hbm), (gv_ref, gv_hbm),
-        ))
-    ]
+    results = (
+        (gtaps_ref, gtaps_hbm), (gh_ref, gh_hbm), (mixed_ref, mixed_hbm), (gq_ref, gq_hbm), (gk_ref, gk_hbm), (gv_ref, gv_hbm),
+    )
+    stores = []
     loads[0].wait()
     for r in range(2):
         note = notes_ref[:, r, :]
@@ -383,8 +391,11 @@
             joined = jnp.concatenate([da[s], note[0][9 + 2 * s : 11 + 2 * s], pad[0:6]], axis=0)
             total = tap[s][0] * da[s] + tap[s][1] * joined[1 : 1 + rows] + tap[s][2] * joined[2 : 2 + rows]
             outputs[s][:, cols] = total.astype(BF16)
-    for store in stores:
-        store.start()
+        for n, (held, result) in enumerate(results):
+            block = (slice(None),) * (len(held.shape) - 1) + (cols,)
+            store = pltpu.make_async_copy(held.at[block], result.at[block], store_sem.at[b, n])
+            store.start()
+            stores.append(store)
     for store in stores:
         store.wait()
 
@@ -417,11 +428,12 @@
             pltpu.VMEM((parts + 1, 2, rows), F32),
             pltpu.VMEM((width, rows), F32),
             pltpu.VMEM((4, parts + 1, chans, rows), F32),
+            pltpu.VMEM((3, 2, parts, chans, rows), F32),
             pltpu.VMEM((3, parts, chans, rows), F32),
             pltpu.VMEM((3, parts, chans, rows), F32),
             pltpu.VMEM((3, width, 2 * rows), F32),
             pltpu.VMEM((3, parts, chans, rows), F32),
-            pltpu.VMEM((width, 6 * rows), BF16),
+            pltpu.VMEM((3, width, 6 * rows), BF16),
             *[pltpu.SemaphoreType.DMA((6,))] * 2,
             *field,
             *wide,
@@ -452,7 +464,7 @@
             *field,
             *taps,
             *wide,
-            pltpu.SemaphoreType.DMA((6,)),
+            pltpu.SemaphoreType.DMA((4, 6)),
             pltpu.VMEM((2, width, rows), F32),
         ],
         compiler_params=pltpu.CompilerParams(vmem_limit_bytes=63 << 20),

time: 58.3 us -> 55.6 us (0.954)
  the two profiles are of different devices: /device:TPU:8 before, /device:TPU:24 now
where the time goes in v4:
time: 55.6 us; the launch traced here: 55.5 us
  Pallas kernels  54.8 us (99%)
  between operations  0.64 us (1%)
    pallas_call x1, Pallas kernels, local(): pl.pallas_call(sequence_kernel, out_shape=(y_all, d_all, notes), in_specs...  51.7 us
    pallas_call x1, Pallas kernels, local(): pl.pallas_call(home_kernel, out_shape=(like, like, like, like, jax.ShapeD...  3.16 us

profile of v4, /device:TPU:24, one launch (start us, length us, event | category | flops | bytes accessed | tf_op | source)
XLA Modules:
  0.0 55.5 jit_solution(6339854648764897774)
XLA Ops:
  0.6 51.7 %sequence_part.1 = (bf16[64,8,128]{2,1,0:T(8,128)(2,1)}, bf16[64,16,128]{2,1,0:T(8,128)(2,1)}, f32[64,2,128]{2,1,0:T(2,128)}) custom-call(bf16[128,512]{1,0:T(8,128)(2,1)} %q_hbm.3, bf16[128,512]{1,0:T(8,128)(2,1)} %k_hbm.3, bf16[128,512]{1,0:T(8,128)(2,1)} %v_hbm.3, bf16[128,512]{1,0:T(8,128)(2,1)} %g_hbm.3, f32[128,512]{1,0:T(8,128)} %h_hbm.1, ...), custom_call_target="tpu_custom_call" | custom-call | tf_op jit(solution)/shard_map/sequence_part/pallas_call | solution.py:415
  52.3 3.2 %home_part.1 = (bf16[128,512]{1,0:T(8,128)(2,1)}, bf16[128,512]{1,0:T(8,128)(2,1)}, bf16[128,512]{1,0:T(8,128)(2,1)}, bf16[128,512]{1,0:T(8,128)(2,1)}, f32[3,3,512]{2,1,0:T(4,128)}, /*index=5*/f32[128,512]{1,0:T(8,128)}) custom-call(bf16[128,512]{1,0:T(8,128)(2,1)} %q_hbm.3, bf16[128,512]{1,0:T(8,128)(2,1)} %k_hbm.3, bf16[128,512]{1,0:T(8,128)(2,1)} %v_hbm.3, ...), custom_call_target="tpu_custom_call" | custom-call | tf_op jit(solution)/shard_map/home_part/pallas_call | solution.py:450

commit v5 on v4

--- a/solution.py
+++ b/solution.py
@@ -79,19 +79,24 @@
         ))
     ]
 
+    def peer_at(i):
+        xi, zi = (i >> 1) & 3, i >> 3
+        x_off = 2 + ((xi + 1) >> 1) * (1 - 2 * (xi & 1))
+        z_off = 4 + ((zi + 1) >> 1) * (1 - 2 * (zi & 1))
+        x_to = ((me >> 4) + x_off) & 3
+        y_to = ((me >> 3) & 1) ^ (1 - (i & 1))
+        z_to = (me + z_off) & 7
+        return (x_to << 4) | (y_to << 3) | z_to
+
+    def span(start, stop, body):
+        def step(i, carry):
+            body(peer_at(i))
+            return carry
+
+        lax.fori_loop(start, stop, step, 0, unroll=9)
+
     def peers(body):
-        def step(i, carry):
-            xi, zi = (i >> 1) & 3, i >> 3
-            x_off = 2 + jnp.where((xi & 1) == 1, -((xi + 1) >> 1), xi >> 1)
-            z_off = 4 + jnp.where((zi & 1) == 1, -((zi + 1) >> 1), zi >> 1)
-            y_off = 1 - (i & 1)
-            x_to = ((me >> 4) + x_off) & 3
-            y_to = ((me >> 3) & 1) ^ y_off
-            z_to = (me + z_off) & 7
-            body((x_to << 4) | (y_to << 3) | z_to)
-            return carry
-
-        lax.fori_loop(0, parts - 1, step, 0)
+        span(0, parts - 1, body)
 
     def target(peer):
         return dict(device_id=(peer, tp), device_id_type=pl.DeviceIdType.MESH)
@@ -117,23 +122,25 @@
 
     pl.semaphore_wait(barrier, parts - 1)
 
-    def exchange(moves):
+    def keep(moves):
         for source, result, n, skip in moves:
             pltpu.make_async_copy(source.at[me + skip], result.at[me], recv_sem.at[n]).start()
 
-        def post(peer):
-            for source, result, n, skip in moves:
-                pltpu.make_async_remote_copy(
-                    src_ref=source.at[peer + skip], dst_ref=result.at[me],
-                    send_sem=send_sem.at[n], recv_sem=recv_sem.at[n], **target(peer)
-                ).start()
-
-        peers(post)
+    def post(peer, moves):
+        for source, result, n, skip in moves:
+            pltpu.make_async_remote_copy(
+                src_ref=source.at[peer + skip], dst_ref=result.at[me],
+                send_sem=send_sem.at[n], recv_sem=recv_sem.at[n], **target(peer)
+            ).start()
+
+    def exchange(moves):
+        keep(moves)
+        peers(lambda peer: post(peer, moves))
 
     def arrived(result, n):
         pltpu.make_async_copy(result, result, recv_sem.at[n]).wait()
 
-    exchange([(wave1, got1, 0, 0), (peaks, got_peaks, 1, 0)])
+    exchange([(peaks, got_peaks, 1, 0), (wave1, got1, 0, 0)])
     exchange([(wave2, got2, 2, 0)])
     arrived(got1, 0)
     arrived(got_peaks, 1)
@@ -278,8 +285,6 @@
         return carry
 
     lax.fori_loop(0, parts // chunk, code_d, 0, unroll=True)
-    exchange([(d_out, d_in, 4, 0)])
-
     group = lax.broadcasted_iota(jnp.int32, (1, chans, rows), 2) // SLOTS
     sublane = lax.broadcasted_iota(jnp.int32, (1, chans, rows), 1)
 
@@ -311,7 +316,10 @@
         notes_out[there, 1:2, :] = flattened(placed(a, 0))
         return tuple(sums)
 
-    sums = lax.fori_loop(0, parts // chunk, tally, (jnp.zeros((chans, rows), F32),) * 9, unroll=2)
+    sums = (jnp.zeros((chans, rows), F32),) * 9
+    d_moves = [(d_out, d_in, 4, 0)]
+    for i in range(parts // chunk):
+        sums = tally(i, sums)
     notes_out[parts, 0:1, :] = jnp.zeros((1, rows), F32)
     lane2 = lane[0]
     first_note = jnp.zeros((chans, rows), F32)
@@ -324,7 +332,9 @@
     later = pl.ds(1, parts)
     notes_out[later] = notes_out[later] + both
 
-    exchange([(notes_out, notes, 5, 1)])
+    note_moves = [(notes_out, notes, 5, 1)]
+    peers(lambda peer: post(peer, note_moves + d_moves))
+    keep(d_moves + note_moves)
     arrived(y_in, 3)
     arrived(d_in, 4)
     arrived(notes, 5)

time: 55.6 us -> 54.4 us (0.978)
  Pallas kernels: 54.8 us -> 53.6 us
    pallas_call x1, Pallas kernels: 51.7 us -> 50.5 us  [local(): pl.pallas_call(sequence_kernel, out_shape=(y_all, d_all, notes), in_specs...]
where the time goes in v5:
time: 54.4 us; the launch traced here: 54.3 us
  Pallas kernels  53.6 us (99%)
  between operations  0.64 us (1%)
    pallas_call x1, Pallas kernels, local(): pl.pallas_call(sequence_kernel, out_shape=(y_all, d_all, notes), in_specs...  50.5 us
    pallas_call x1, Pallas kernels, local(): pl.pallas_call(home_kernel, out_shape=(like, like, like, like, jax.ShapeD...  3.16 us

profile of v5, /device:TPU:24, one launch (start us, length us, event | category | flops | bytes accessed | tf_op | source)
XLA Modules:
  0.0 54.3 jit_solution(3635471943992937136)
XLA Ops:
  0.6 50.5 %sequence_part.1 = (bf16[64,8,128]{2,1,0:T(8,128)(2,1)}, bf16[64,16,128]{2,1,0:T(8,128)(2,1)}, f32[64,2,128]{2,1,0:T(2,128)}) custom-call(bf16[128,512]{1,0:T(8,128)(2,1)} %q_hbm.3, bf16[128,512]{1,0:T(8,128)(2,1)} %k_hbm.3, bf16[128,512]{1,0:T(8,128)(2,1)} %v_hbm.3, bf16[128,512]{1,0:T(8,128)(2,1)} %g_hbm.3, f32[128,512]{1,0:T(8,128)} %h_hbm.1, ...), custom_call_target="tpu_custom_call" | custom-call | tf_op jit(solution)/shard_map/sequence_part/pallas_call | solution.py:425
  51.1 3.2 %home_part.1 = (bf16[128,512]{1,0:T(8,128)(2,1)}, bf16[128,512]{1,0:T(8,128)(2,1)}, bf16[128,512]{1,0:T(8,128)(2,1)}, bf16[128,512]{1,0:T(8,128)(2,1)}, f32[3,3,512]{2,1,0:T(4,128)}, /*index=5*/f32[128,512]{1,0:T(8,128)}) custom-call(bf16[128,512]{1,0:T(8,128)(2,1)} %q_hbm.3, bf16[128,512]{1,0:T(8,128)(2,1)} %k_hbm.3, bf16[128,512]{1,0:T(8,128)(2,1)} %v_hbm.3, ...), custom_call_target="tpu_custom_call" | custom-call | tf_op jit(solution)/shard_map/home_part/pallas_call | solution.py:460

commit v6 on v5

--- a/solution.py
+++ b/solution.py
@@ -101,8 +101,10 @@
     def target(peer):
         return dict(device_id=(peer, tp), device_id_type=pl.DeviceIdType.MESH)
 
+    for load in loads[:6]:
+        load.start()
     peers(lambda peer: pl.semaphore_signal(barrier, inc=1, **target(peer)))
-    for load in loads:
+    for load in loads[6:]:
         load.start()
 
     for load in loads[:6]:

time: 54.4 us -> 54.4 us (level)
  no operation moved by 1% of the time
where the time goes in v6:
time: 54.4 us; the launch traced here: 54.3 us
  Pallas kernels  53.6 us (99%)
  between operations  0.64 us (1%)
    pallas_call x1, Pallas kernels, local(): pl.pallas_call(sequence_kernel, out_shape=(y_all, d_all, notes), in_specs...  50.5 us
    pallas_call x1, Pallas kernels, local(): pl.pallas_call(home_kernel, out_shape=(like, like, like, like, jax.ShapeD...  3.16 us

profile of v6, /device:TPU:24, one launch (start us, length us, event | category | flops | bytes accessed | tf_op | source)
XLA Modules:
  0.0 54.3 jit_solution(14097303128894986329)
XLA Ops:
  0.6 50.5 %sequence_part.1 = (bf16[64,8,128]{2,1,0:T(8,128)(2,1)}, bf16[64,16,128]{2,1,0:T(8,128)(2,1)}, f32[64,2,128]{2,1,0:T(2,128)}) custom-call(bf16[128,512]{1,0:T(8,128)(2,1)} %q_hbm.3, bf16[128,512]{1,0:T(8,128)(2,1)} %k_hbm.3, bf16[128,512]{1,0:T(8,128)(2,1)} %v_hbm.3, bf16[128,512]{1,0:T(8,128)(2,1)} %g_hbm.3, f32[128,512]{1,0:T(8,128)} %h_hbm.1, ...), custom_call_target="tpu_custom_call" | custom-call | tf_op jit(solution)/shard_map/sequence_part/pallas_call | solution.py:427
  51.1 3.2 %home_part.1 = (bf16[128,512]{1,0:T(8,128)(2,1)}, bf16[128,512]{1,0:T(8,128)(2,1)}, bf16[128,512]{1,0:T(8,128)(2,1)}, bf16[128,512]{1,0:T(8,128)(2,1)}, f32[3,3,512]{2,1,0:T(4,128)}, /*index=5*/f32[128,512]{1,0:T(8,128)}) custom-call(bf16[128,512]{1,0:T(8,128)(2,1)} %q_hbm.3, bf16[128,512]{1,0:T(8,128)(2,1)} %k_hbm.3, bf16[128,512]{1,0:T(8,128)(2,1)} %v_hbm.3, ...), custom_call_target="tpu_custom_call" | custom-call | tf_op jit(solution)/shard_map/home_part/pallas_call | solution.py:462

commit v7 on v6

--- a/solution.py
+++ b/solution.py
@@ -374,6 +374,14 @@
     for load in loads[1:]:
         load.wait()
     row = lax.broadcasted_iota(jnp.int32, (rows, rows), 0)
+
+    def put(b, n):
+        held, result = results[n]
+        block = (slice(None),) * (len(held.shape) - 1) + (slice(b * rows, (b + 1) * rows),)
+        store = pltpu.make_async_copy(held.at[block], result.at[block], store_sem.at[b, n])
+        store.start()
+        stores.append(store)
+
     inputs = (q_ref, k_ref, v_ref)
     outputs = (gq_ref, gk_ref, gv_ref)
     pad = jnp.zeros((8, rows), F32)
@@ -388,7 +396,9 @@
             jnp.transpose(value.reshape(rows, rows)) * (note[1][6 + o : 7 + o] * (1.0 / RANGE))
             for o, value in enumerate((decode(y_ref[groups].astype(F32)), pair[:, 0:8], pair[:, 8:16]))
         ]
+        put(b, 0)
         gh_ref[:, cols] = dh
+        put(b, 1)
         tap = [[taps_ref[s, j : j + 1, cols] for j in range(3)] for s in range(3)]
         a = []
         for s in range(3):
@@ -398,16 +408,13 @@
             total = jnp.where(row == 0, note[1][2 * s : 2 * s + 1], total)
             a.append(jnp.where(row == 1, note[1][2 * s + 1 : 2 * s + 2], total))
         mixed_ref[:, cols] = (a[1] * y).astype(BF16)
+        put(b, 2)
         da = [dz * a[2], g_ref[:, cols].astype(F32) * y, dz * a[0]]
         for s in range(3):
             joined = jnp.concatenate([da[s], note[0][9 + 2 * s : 11 + 2 * s], pad[0:6]], axis=0)
             total = tap[s][0] * da[s] + tap[s][1] * joined[1 : 1 + rows] + tap[s][2] * joined[2 : 2 + rows]
             outputs[s][:, cols] = total.astype(BF16)
-        for n, (held, result) in enumerate(results):
-            block = (slice(None),) * (len(held.shape) - 1) + (cols,)
-            store = pltpu.make_async_copy(held.at[block], result.at[block], store_sem.at[b, n])
-            store.start()
-            stores.append(store)
+            put(b, 3 + s)
     for store in stores:
         store.wait()
 

time: 54.4 us -> 54.4 us (level)
  no operation moved by 1% of the time
where the time goes in v7:
time: 54.4 us; the launch traced here: 54.3 us
  Pallas kernels  53.6 us (99%)
  between operations  0.64 us (1%)
    pallas_call x1, Pallas kernels, local(): pl.pallas_call(sequence_kernel, out_shape=(y_all, d_all, notes), in_specs...  50.5 us
    pallas_call x1, Pallas kernels, local(): pl.pallas_call(home_kernel, out_shape=(like, like, like, like, jax.ShapeD...  3.16 us

profile of v7, /device:TPU:24, one launch (start us, length us, event | category | flops | bytes accessed | tf_op | source)
XLA Modules:
  0.0 54.3 jit_solution(14097303128894986329)
XLA Ops:
  0.6 50.5 %sequence_part.1 = (bf16[64,8,128]{2,1,0:T(8,128)(2,1)}, bf16[64,16,128]{2,1,0:T(8,128)(2,1)}, f32[64,2,128]{2,1,0:T(2,128)}) custom-call(bf16[128,512]{1,0:T(8,128)(2,1)} %q_hbm.3, bf16[128,512]{1,0:T(8,128)(2,1)} %k_hbm.3, bf16[128,512]{1,0:T(8,128)(2,1)} %v_hbm.3, bf16[128,512]{1,0:T(8,128)(2,1)} %g_hbm.3, f32[128,512]{1,0:T(8,128)} %h_hbm.1, ...), custom_call_target="tpu_custom_call" | custom-call | tf_op jit(solution)/shard_map/sequence_part/pallas_call | solution.py:434
  51.1 3.2 %home_part.1 = (bf16[128,512]{1,0:T(8,128)(2,1)}, bf16[128,512]{1,0:T(8,128)(2,1)}, bf16[128,512]{1,0:T(8,128)(2,1)}, bf16[128,512]{1,0:T(8,128)(2,1)}, f32[3,3,512]{2,1,0:T(4,128)}, /*index=5*/f32[128,512]{1,0:T(8,128)}) custom-call(bf16[128,512]{1,0:T(8,128)(2,1)} %q_hbm.3, bf16[128,512]{1,0:T(8,128)(2,1)} %k_hbm.3, bf16[128,512]{1,0:T(8,128)(2,1)} %v_hbm.3, ...), custom_call_target="tpu_custom_call" | custom-call | tf_op jit(solution)/shard_map/home_part/pallas_call | solution.py:469
